TPU v7x, 256 devices: a whole 4x4x8 slice. The times are simulated.
256 devices in a mesh: row: 8 (over y_hi, x), col: 32 (over z, y_lo, core).
Axes of the slice: x: 4, y: 4 (y_hi: 2, y_lo: 2; y = y_hi * 2 + y_lo), z: 8, core: 2. Of those that a mesh axis runs over, the one named last changes fastest.
Arguments:
- features: bfloat16 [65536, 128], P(('row', 'col')), may hold values from -6 to 6
- labels: int32 [65536], P(('row', 'col')), may hold values from 0 to 127
- train_mask: int32 [65536], P(('row', 'col')), may hold values from 0 to 1
- adj_rows: int32 [8, 32, 192], P('row', 'col'), may hold values from 0 to 15, as said below
- adj_cols: int32 [8, 32, 192], P('row', 'col'), may hold values from 0 to 63, as said below
- adj_live: int32 [8, 32], P('row', 'col'), may hold values from 1 to 192, as said below
- adj_values: bfloat16 [8, 32, 192, 128, 128], P('row', 'col'), may hold values from -0.0390625 to 0.0390625
- w_first: bfloat16 [128, 256], replicated, may hold values from -0.5 to 0.5
- b_first: float32 [256], replicated, may hold values from -0.5 to 0.5
- w_second: bfloat16 [256, 128], replicated, may hold values from -0.375 to 0.375
- b_second: float32 [128], replicated, may hold values from -1 to 1
Outputs:
- logits: bfloat16 [65536, 128], P(('row', 'col'))
- loss_value: float32 [], replicated
- grad_w_first: float32 [128, 256], replicated
- grad_b_first: float32 [256], replicated
- grad_w_second: float32 [256, 128], replicated
- grad_b_second: float32 [128], replicated
Inputs may be any that keep to these rules, and one draw needn't show every extreme that they name: Within one tile the 192 positions (adj_rows, adj_cols) are distinct. Within one tile the 192 positions (adj_rows, adj_cols) are distinct. `adj_live`: some tile has all 192 blocks live.
All inputs are finite; a program needn't handle non-finite values.
Results may differ from a plain program's by a relative error of at most 0.015.
Values may be sent and summed in bfloat16 or wider, within the bound.
A program may use at most 128 MiB of HBM per device.

v0:
```python
import jax
import jax.numpy as jnp
from jax import lax
from jax.sharding import PartitionSpec as P

highest = lax.Precision.HIGHEST


def tile_forward(blocks, row_ids, col_ids, gathered, out_blocks):
    block_size = blocks.shape[-1]
    feat_width = gathered.shape[1]
    sources = jnp.take(gathered.reshape(-1, block_size, feat_width), col_ids, axis=0)
    products = jnp.einsum(
        "kab,kbf->kaf", blocks, sources, preferred_element_type=jnp.float32, precision=highest
    )
    placing = (jnp.arange(out_blocks, dtype=jnp.int32)[:, None] == row_ids[None, :]).astype(
        jnp.float32
    )
    summed = jnp.einsum("ik,kaf->iaf", placing, products, precision=highest)
    return summed.reshape(out_blocks * block_size, feat_width)


def tile_backward(blocks, row_ids, col_ids, gathered, out_blocks):
    block_size = blocks.shape[-1]
    feat_width = gathered.shape[1]
    sources = jnp.take(gathered.reshape(-1, block_size, feat_width), row_ids, axis=0)
    products = jnp.einsum(
        "kab,kaf->kbf", blocks, sources, preferred_element_type=jnp.float32, precision=highest
    )
    placing = (jnp.arange(out_blocks, dtype=jnp.int32)[:, None] == col_ids[None, :]).astype(
        jnp.float32
    )
    summed = jnp.einsum("jk,kbf->jbf", placing, products, precision=highest)
    return summed.reshape(out_blocks * block_size, feat_width)


def local(
    features,
    labels,
    train_mask,
    adj_rows,
    adj_cols,
    adj_live,
    adj_values,
    w_first,
    b_first,
    w_second,
    b_second,
):
    node_count = features.shape[0]
    block_size = adj_values.shape[-1]
    row_blocks = lax.axis_size("row") * node_count // block_size
    col_blocks = lax.axis_size("col") * node_count // block_size
    row_ids = adj_rows[0, 0]
    col_ids = adj_cols[0, 0]
    live_mask = (jnp.arange(row_ids.shape[0], dtype=jnp.int32) < adj_live[0, 0]).astype(
        jnp.bfloat16
    )
    blocks = adj_values[0, 0] * live_mask[:, None, None]
    w_second_wide = w_second.astype(jnp.float32)
    gathered = lax.all_gather(features, "col", axis=0, tiled=True)
    agg_in = lax.psum_scatter(
        tile_forward(blocks, row_ids, col_ids, gathered, row_blocks),
        "row",
        scatter_dimension=0,
        tiled=True,
    )
    pre_hidden = (
        jnp.dot(
            agg_in,
            w_first.astype(jnp.float32),
            precision=highest,
            preferred_element_type=jnp.float32,
        )
        + b_first
    )
    hidden = jax.nn.relu(pre_hidden).astype(jnp.bfloat16)
    hidden_strip = lax.all_gather(hidden, "col", axis=0, tiled=True)
    agg_hidden = lax.psum_scatter(
        tile_forward(blocks, row_ids, col_ids, hidden_strip, row_blocks),
        "row",
        scatter_dimension=0,
        tiled=True,
    )
    scores = (
        jnp.dot(agg_hidden, w_second_wide, precision=highest, preferred_element_type=jnp.float32)
        + b_second
    )
    row_max = jnp.max(scores, axis=1, keepdims=True)
    log_total = jnp.log(jnp.sum(jnp.exp(scores - row_max), axis=1, keepdims=True)) + row_max
    onehot = (jnp.arange(scores.shape[1], dtype=jnp.int32)[None, :] == labels[:, None]).astype(
        jnp.float32
    )
    picked = jnp.sum(onehot * scores, axis=1)
    mask_float = train_mask.astype(jnp.float32)
    loss_sum = lax.psum(jnp.sum(mask_float * (log_total[:, 0] - picked)), ("row", "col"))
    train_count = jnp.float32(node_count * lax.axis_size("row") * lax.axis_size("col") // 2)
    loss_value = loss_sum / train_count
    d_scores = mask_float[:, None] * (jnp.exp(scores - log_total) - onehot) / train_count
    grad_b_second = jnp.sum(d_scores, axis=0)
    d_agg = jnp.dot(
        d_scores, w_second_wide.T, precision=highest, preferred_element_type=jnp.float32
    )
    grad_strip = lax.all_gather(d_agg, "row", axis=0, tiled=True)
    d_hidden = lax.psum_scatter(
        tile_backward(blocks, row_ids, col_ids, grad_strip, col_blocks),
        "col",
        scatter_dimension=0,
        tiled=True,
    )
    grad_w_second = jnp.dot(
        agg_hidden.T, d_scores, precision=highest, preferred_element_type=jnp.float32
    )
    d_pre = jnp.where(pre_hidden > 0, d_hidden, jnp.zeros_like(d_hidden))
    grad_w_first = jnp.dot(agg_in.T, d_pre, precision=highest, preferred_element_type=jnp.float32)
    grad_b_first = jnp.sum(d_pre, axis=0)
    grad_w_first, grad_b_first, grad_w_second, grad_b_second = lax.psum(
        (grad_w_first, grad_b_first, grad_w_second, grad_b_second), ("row", "col")
    )
    return (
        scores.astype(jnp.bfloat16),
        loss_value,
        grad_w_first,
        grad_b_first,
        grad_w_second,
        grad_b_second,
    )


def solution(mesh):
    in_specs = (
        P(("row", "col"), None),
        P(("row", "col")),
        P(("row", "col")),
        P("row", "col", None),
        P("row", "col", None),
        P("row", "col"),
        P("row", "col", None, None, None),
        P(),
        P(),
        P(),
        P(),
    )
    out_specs = (P(("row", "col"), None), P(), P(), P(), P(), P())
    return jax.shard_map(local, mesh=mesh, in_specs=in_specs, out_specs=out_specs, check_vma=False)
```

profile of v0, /device:TPU:1, one launch (start us, length us, event | category | flops | bytes accessed | tf_op | source)
XLA Modules:
  0.0 934.8 jit_solution(1708452295760395478)
XLA Ops:
  10.0 68.8 %all-gather.4.cloned.1.call-done = bf16[8192,128]{1,0:T(8,128)(2,1)} async-done(((bf16[256,128]{1,0:T(8,128)(2,1)}), bf16[8192,128]{1,0:T(8,128)(2,1)}) %all-gather.4.cloned.1.call-update) | async-done | bytes 2097168 | tf_op jit(solution)/shard_map/all_gather | solution.py:61
  78.8 9.6 %gather_fusion = bf16[192,128,128]{2,1,0:T(8,128)(2,1)} fusion(bf16[64,128,128]{2,1,0:T(8,128)(2,1)} %bitcast.38, s32[1024]{0:T(1024)S(1)} %pad_clamp_fusion.1), kind=kCustom, calls=%fused_computation | custom fusion | bytes 12583680 | tf_op jit(solution)/shard_map/jit(_take)/gather | solution.py:12
  88.4 11.0 %fusion.14 = f32[192,128,128]{2,1,0:T(8,128)} fusion(bf16[192,128,128]{2,1,0:T(8,128)(2,1)} %gather_fusion, pred[192]{0:T(512)(128)(4,1)S(1)} %get-tuple-element.30, bf16[1,1,192,128,128]{4,3,2,1,0:T(8,128)(2,1)} %param.17, bf16[192]{0:T(256)(128)(2,1)S(1)} %get-tuple-element.31), kind=kOutput, calls=%fused_computation.18 | convolution fusion | flops 811597824 | bytes 25166400 | tf_op jit(solution)/shard_map/kab,kbf->kaf/dot_general | solution.py:13
  99.4 15.3 %fusion.6 = f32[16,128,128]{2,0,1:T(8,128)S(1)} fusion(f32[192,128,128]{2,1,0:T(8,128)} %fusion.14, s32[192]{0:T(256)S(1)} %bitcast.43), kind=kOutput, calls=%fused_computation.9 | convolution fusion | flops 603982848 | bytes 13632256 | tf_op jit(solution)/shard_map/ik,kaf->iaf/dot_general | solution.py:19
  114.7 1.3 copy.19
  116.1 74.6 %reduce-scatter.4.cloned.1.call-done = f32[256,128]{1,0:T(8,128)} async-done(((f32[2048,128]{1,0:T(8,128)}), f32[256,128]{1,0:T(8,128)}) %reduce-scatter.4.cloned.1.call-update) | async-done | bytes 131088 | tf_op jit(solution)/shard_map/reduce_scatter | solution.py:62
  190.7 1.8 maximum_convert_fusion
  193.0 68.6 %all-gather.6.cloned.1.call-done = bf16[8192,256]{1,0:T(8,128)(2,1)} async-done(((bf16[256,256]{1,0:T(8,128)(2,1)}), bf16[8192,256]{1,0:T(8,128)(2,1)}) %all-gather.6.cloned.1.call-update) | async-done | bytes 4194320 | tf_op jit(solution)/shard_map/all_gather | solution.py:78
  261.5 10.5 %gather_fusion.1 = bf16[192,128,256]{2,1,0:T(8,128)(2,1)} fusion(bf16[64,128,256]{2,1,0:T(8,128)(2,1)} %bitcast.36, s32[1024]{0:T(1024)S(1)} %pad_clamp_fusion.1), kind=kCustom, calls=%fused_computation.1 | custom fusion | bytes 25166592 | tf_op jit(solution)/shard_map/jit(_take)/gather | solution.py:12
  272.0 13.8 %fusion.9 = f32[192,128,256]{2,1,0:T(8,128)} fusion(bf16[192,128,256]{2,1,0:T(8,128)(2,1)} %gather_fusion.1, pred[192]{0:T(512)(128)(4,1)S(1)} %get-tuple-element.30, bf16[1,1,192,128,128]{4,3,2,1,0:T(8,128)(2,1)} %param.17, bf16[192]{0:T(256)(128)(2,1)S(1)} %get-tuple-element.31), kind=kOutput, calls=%fused_computation.12 | convolution fusion | flops 1620049920 | bytes 44040768 | tf_op jit(solution)/shard_map/kab,kbf->kaf/dot_general | solution.py:13
  285.9 29.5 %fusion.2 = f32[16,128,256]{2,0,1:T(8,128)S(1)} fusion(f32[192,128,256]{2,1,0:T(8,128)} %fusion.9, s32[192]{0:T(256)S(1)} %bitcast.44), kind=kOutput, calls=%fused_computation.5 | convolution fusion | flops 1207962624 | bytes 27263744 | tf_op jit(solution)/shard_map/ik,kaf->iaf/dot_general | solution.py:19
  315.4 2.6 copy.20
  318.0 78.3 %reduce-scatter.6.cloned.1.call-done = f32[256,256]{1,0:T(8,128)} async-done(((f32[2048,256]{1,0:T(8,128)}), f32[256,256]{1,0:T(8,128)}) %reduce-scatter.6.cloned.1.call-update) | async-done | bytes 262160 | tf_op jit(solution)/shard_map/reduce_scatter | solution.py:79
  398.8 59.2 %all-gather.8.cloned.1.call-done = f32[2048,256]{1,0:T(8,128)} async-done(((f32[256,256]{1,0:T(8,128)}), f32[2048,256]{1,0:T(8,128)}) %all-gather.8.cloned.1.call-update) | async-done | bytes 2097168 | tf_op jit(solution)/shard_map/all_gather | solution.py:104
  458.0 14.0 %gather_fusion.2 = f32[192,128,256]{2,1,0:T(8,128)} fusion(f32[16,128,256]{2,1,0:T(8,128)} %bitcast.35, s32[1024]{0:T(1024)S(1)} %pad_clamp_fusion), kind=kCustom, calls=%fused_computation.2 | custom fusion | bytes 50332416 | tf_op jit(solution)/shard_map/jit(_take)/gather | solution.py:26
  471.9 26.4 %fusion.4 = f32[192,128,256]{2,1,0:T(8,128)} fusion(f32[192,128,256]{2,1,0:T(8,128)} %gather_fusion.2, pred[192]{0:T(512)(128)(4,1)S(1)} %compare_and_fusion, bf16[1,1,192,128,128]{4,3,2,1,0:T(8,128)(2,1)} %param.17, bf16[192]{0:T(256)(128)(2,1)S(1)} %get-tuple-element.31), kind=kOutput, calls=%fused_computation.7 | convolution fusion | flops 9673113600 | bytes 56623680 | tf_op jit(solution)/shard_map/kab,kaf->kbf/dot_general | solution.py:27
  498.3 32.1 %fusion = f32[64,128,256]{2,0,1:T(8,128)S(1)} fusion(f32[192,128,256]{2,1,0:T(8,128)} %fusion.4, s32[192]{0:T(256)S(1)} %bitcast.42), kind=kOutput, calls=%fused_computation.3 | convolution fusion | flops 4831850496 | bytes 33555200 | tf_op jit(solution)/shard_map/jk,kbf->jbf/dot_general | solution.py:33
  530.4 8.1 copy.21
  541.3 124.1 %reduce-scatter.8.cloned.1.call-done = f32[256,256]{1,0:T(8,128)} async-done(((f32[8192,256]{1,0:T(8,128)}), f32[256,256]{1,0:T(8,128)}) %reduce-scatter.8.cloned.1.call-update) | async-done | bytes 262160 | tf_op jit(solution)/shard_map/reduce_scatter | solution.py:105
  665.4 2.0 fusion.22
  668.5 80.8 %all-reduce = (f32[]{:T(128)}, f32[256]{0:T(256)}, f32[128]{0:T(128)}) all-reduce(f32[]{:T(128)} %multiply_reduce_fusion, f32[256]{0:T(256)S(1)} %fusion.21, f32[128]{0:T(128)S(1)} %get-tuple-element.18), channel_id=1, replica_groups=mesh['row'=8,'col'=32] {'row','col'}, use_global_device_ids=true, to_apply=%region_6.7 | all-reduce | flops 385 | bytes 3080 | tf_op jit(solution)/shard_map/psum | solution.py:96
  750.0 173.3 %all-reduce.4.cloned.1.call-done = (f32[128,256]{1,0:T(8,128)}, f32[256,128]{1,0:T(8,128)}) async-done(((f32[128,256]{1,0:T(8,128)}, f32[256,128]{1,0:T(8,128)}), (f32[128,256]{1,0:T(8,128)}, f32[256,128]{1,0:T(8,128)})) %all-reduce.4.cloned.1.call-update) | async-done | bytes 262160 | tf_op jit(solution)/shard_map/psum | solution.py:117
  923.3 1.6 copy.35
  924.9 1.6 copy.36
  (52 shorter events, 9.0 us)
Async XLA Ops:
  7.2 183.6 %copy-start = (bf16[128,256]{1,0:T(8,128)(2,1)S(1)}, bf16[128,256]{1,0:T(8,128)(2,1)}, u32[]{:S(2)}) copy-start(bf16[128,256]{1,0:T(8,128)(2,1)} %param.18) | copy-start | bytes 196612
  7.2 71.6 %all-gather.4.cloned.1.call-start = ((), (), s32[]{:S(2)}) async-start(), calls=%async_computation.3 | async-start | bytes 2162688 | tf_op jit(solution)/shard_map/all_gather | solution.py:61
  7.9 182.8 %reduce-scatter.4.cloned.1.call-start = ((), (), s32[]{:S(2)}) async-start(), calls=%async_computation.4 | async-start | bytes 1179648 | tf_op jit(solution)/shard_map/reduce_scatter | solution.py:62
  88.4 11.0 %copy-start.7 = (s32[1,1,192]{2,1,0:T(1,128)S(1)}, s32[1,1,192]{2,1,0:T(1,128)}, u32[]{:S(2)}) copy-start(s32[1,1,192]{2,1,0:T(1,128)} %param.14) | copy-start | bytes 2308
  99.4 91.3 %copy-start.9 = (f32[256]{0:T(256)S(1)}, f32[256]{0:T(256)}, u32[]{:S(2)}) copy-start(f32[256]{0:T(256)} %param.19) | copy-start | bytes 3076
  116.0 145.5 %all-gather.6.cloned.1.call-start = ((), (), s32[]{:S(2)}) async-start(), calls=%async_computation.5 | async-start | bytes 4325376 | tf_op jit(solution)/shard_map/all_gather | solution.py:78
  192.6 203.7 %reduce-scatter.6.cloned.1.call-start = ((), (), s32[]{:S(2)}) async-start(), calls=%async_computation.6 | async-start | bytes 2359296 | tf_op jit(solution)/shard_map/reduce_scatter | solution.py:79
  285.9 32.1 %copy-start.8 = (s32[256]{0:T(256)S(1)}, s32[256]{0:T(256)}, u32[]{:S(2)}) copy-start(s32[256]{0:T(256)} %param.13) | copy-start | bytes 3076
  285.9 110.4 %copy-start.4 = (bf16[256,128]{1,0:T(8,128)(2,1)S(1)}, bf16[256,128]{1,0:T(8,128)(2,1)}, u32[]{:S(2)}) copy-start(bf16[256,128]{1,0:T(8,128)(2,1)} %param.20) | copy-start | bytes 196612
  285.9 110.4 %copy-start.10 = (f32[128]{0:T(128)S(1)}, f32[128]{0:T(128)}, u32[]{:S(2)}) copy-start(f32[128]{0:T(128)} %param.21) | copy-start | bytes 1540
  285.9 111.8 %copy-start.6 = (s32[256]{0:T(256)S(1)}, s32[256]{0:T(256)}, u32[]{:S(2)}) copy-start(s32[256]{0:T(256)} %param.12) | copy-start | bytes 3076
  318.0 140.0 %all-gather.8.cloned.1.call-start = ((), (), s32[]{:S(2)}) async-start(), calls=%async_computation.7 | async-start | bytes 2359296 | tf_op jit(solution)/shard_map/all_gather | solution.py:104
  398.7 266.7 %reduce-scatter.8.cloned.1.call-start = ((), (), s32[]{:S(2)}) async-start(), calls=%async_computation.8 | async-start | bytes 8650752 | tf_op jit(solution)/shard_map/reduce_scatter | solution.py:105
  471.9 26.4 %copy-start.5 = (s32[1,1,192]{2,1,0:T(1,128)S(1)}, s32[1,1,192]{2,1,0:T(1,128)}, u32[]{:S(2)}) copy-start(s32[1,1,192]{2,1,0:T(1,128)} %param.15) | copy-start | bytes 2308
  530.4 396.0 %copy-start.1 = (bf16[128,256]{1,0:T(8,128)(2,1)S(1)}, bf16[128,256]{1,0:T(8,128)(2,1)}, u32[]{:S(2)}) copy-start(bf16[128,256]{1,0:T(8,128)(2,1)} %param.18) | copy-start | bytes 196612
  538.5 1.6 copy-start.2
  538.5 126.9 %copy-start.3 = (f32[256,128]{1,0:T(8,128)S(1)}, f32[256,128]{1,0:T(8,128)}, u32[]{:S(2)}) copy-start(f32[256,128]{1,0:T(8,128)} %reduce-scatter.4.cloned.1.call-done) | copy-start | bytes 393220
  538.6 384.7 %all-reduce.4.cloned.1.call-start = ((), (), s32[]{:S(2)}) async-start(), calls=%async_computation.9 | async-start | bytes 524288 | tf_op jit(solution)/shard_map/psum | solution.py:117
Sparse Core Ops, SparseCore 0:
  9.9 68.8 all-gather.3
  116.2 74.5 reduce-scatter.3
  193.3 68.1 all-gather.5
  318.1 78.1 reduce-scatter.5
  398.8 59.0 all-gather.7
  538.7 126.7 reduce-scatter.7
  671.6 251.6 all-reduce.3
where the time goes:
time: 944 us; the launch traced here: 935 us
  waiting for transfers between devices  648 us (69%)
  matrix products  135 us (14%)
  blocking collectives  80.8 us (9%)
  local copies, waits for them, and re-layouts  49.9 us (5%)
  between operations  17.1 us (2%)
    psum x1, waiting for transfers between devices, local(): lax.psum((grad_w_first, grad_b_first, grad_w_second, grad_b_second), ('ro...  173 us
    reduce_scatter x1, waiting for transfers between devices, local(): lax.psum_scatter(tile_backward(blocks, row_ids, col_ids, grad_strip, col_...  124 us
    psum x1, blocking collectives, local(): lax.psum(jnp.sum(mask_float * (log_total[:, 0] - picked)), ('row', 'col'))  80.8 us
    reduce_scatter x1, waiting for transfers between devices, local(): lax.psum_scatter(tile_forward(blocks, row_ids, col_ids, hidden_strip, row...  78.3 us
    reduce_scatter x1, waiting for transfers between devices, local(): lax.psum_scatter(tile_forward(blocks, row_ids, col_ids, gathered, row_blo...  74.6 us
    all_gather x1, waiting for transfers between devices, local(): gathered = lax.all_gather(features, 'col', axis=0, tiled=True)  68.8 us
    all_gather x1, waiting for transfers between devices, local(): hidden_strip = lax.all_gather(hidden, 'col', axis=0, tiled=True)  68.6 us
    all_gather x1, waiting for transfers between devices, local(): grad_strip = lax.all_gather(d_agg, 'row', axis=0, tiled=True)  59.2 us
  transfers between devices with their start and end apart: 7, of which 7 were waited for; matrix products, arithmetic and copies ran while one was open for 1% of the time, Pallas kernels for 0%

commit v1 on v0

v1 whole, which is shorter than its diff:
```python
import functools

import jax
import jax.numpy as jnp
from jax import lax
from jax.experimental import pallas as pl
from jax.experimental.pallas import tpu as pltpu
from jax.sharding import PartitionSpec as P

MESH = pl.DeviceIdType.MESH
F32, BF16 = jnp.float32, jnp.bfloat16
ANY = pl.BlockSpec(memory_space=pl.ANY)
VM = pl.BlockSpec(memory_space=pltpu.VMEM)
SM = pl.BlockSpec(memory_space=pltpu.SMEM)
LIMIT = 40 * 1024 * 1024
UNROLL = 8
GROUP = 16


def dot(a, b):
    return jnp.dot(a, b, preferred_element_type=F32)


def dot_nt(a, b):
    return lax.dot_general(a, b, (((1,), (1,)), ((), ())), preferred_element_type=F32)


def halves(a):
    hi = a.astype(BF16)
    return hi, (a - hi.astype(F32)).astype(BF16)


def place():
    r, c = lax.axis_index("row"), lax.axis_index("col")
    return r, c, c // 4, (c // 2) % 2, c % 2


def remote(src, dst, send, recv, r, c):
    return pltpu.make_async_remote_copy(
        src_ref=src, dst_ref=dst, send_sem=send, recv_sem=recv,
        device_id=(r, c), device_id_type=MESH,
    )


def col_neighbours(z, yl, k):
    up, down = (z + 1) % 8, (z + 7) % 8
    return (4 * up + 2 * yl + k, 4 * down + 2 * yl + k, 4 * z + 2 * (1 - yl) + k, 4 * z + 2 * yl + 1 - k)


def row_peers(r):
    x, yh = r % 4, r // 4
    to, came = [], []
    for dy, dx in ((1, 2), (0, 2), (1, 1), (1, 3), (0, 1), (0, 3), (1, 0)):
        y2 = (yh + dy) % 2
        to.append(4 * y2 + (x + dx) % 4)
        came.append(4 * y2 + (x + 4 - dx) % 4)
    return to, came


def greet(devices):
    barrier = pltpu.get_barrier_semaphore()
    for device in devices:
        pl.semaphore_signal(barrier, inc=1, device_id=device, device_id_type=MESH)
    pl.semaphore_wait(barrier, len(devices))


GATHER_SCRATCH = [
    pltpu.SemaphoreType.DMA((32,)),
    pltpu.SemaphoreType.DMA((32,)),
    pltpu.SemaphoreType.DMA,
]


def gather_col(src, out, send, recv, local):
    r, c, z, yl, k = place()
    up, down, across, twin = col_neighbours(z, yl, k)
    started = []

    def slot_of(dz, other):
        return 4 * ((z + dz + 8) % 8) + 2 * (1 - yl if other else yl) + k

    def push(block, slot, to):
        copy = remote(block, out.at[slot], send.at[len(started)], recv.at[slot], r, to)
        copy.start()
        started.append(copy)

    def arrived(slot):
        remote(src, out.at[slot], send.at[0], recv.at[slot], r, twin).wait_recv()

    for to in (across, up, down, twin):
        push(src, c, to)
    mine = pltpu.make_async_copy(src, out.at[c], local)
    mine.start()
    beside = slot_of(0, True)
    arrived(beside)
    for to in (up, down, twin):
        push(out.at[beside], beside, to)
    for step in range(1, 5):
        for other, rising in ((False, True), (False, False), (True, True), (True, False)):
            reach = 4 if other != rising else 3
            if step > reach:
                continue
            slot = slot_of(-step if rising else step, other)
            arrived(slot)
            if step < reach:
                push(out.at[slot], slot, up if rising else down)
            push(out.at[slot], slot, twin)
    for dz in range(8):
        for other in (False, True):
            far = slot_of(dz, other)
            arrived(far + 1 - 2 * k)
    for copy in started:
        copy.wait_send()
    mine.wait()


def gather_kernel(src, out, send, recv, local):
    r, c, z, yl, k = place()
    greet([(r, n) for n in col_neighbours(z, yl, k)])
    gather_col(src, out, send, recv, local)


def gather_call(features):
    return pl.pallas_call(
        gather_kernel,
        out_shape=jax.ShapeDtypeStruct((32,) + features.shape, BF16),
        in_specs=[ANY],
        out_specs=ANY,
        scratch_shapes=GATHER_SCRATCH,
        compiler_params=pltpu.CompilerParams(collective_id=0, has_side_effects=True, vmem_limit_bytes=LIMIT),
        name="gather_features",
    )(features)


def product_kernel(backward, rows, cols, live, blocks, source, out, held, total, sem):
    n = live[0, 0]
    loads = (n + GROUP - 1) // GROUP

    def load(g):
        part = pl.ds(g * GROUP, GROUP)
        return pltpu.make_async_copy(blocks.at[part], held.at[part], sem.at[g])

    @pl.loop(0, loads)
    def _(g):
        load(g).start()

    outs = total.shape[0] - 1

    @pl.loop(0, outs)
    def _(i):
        total[i] = jnp.zeros(total.shape[1:], F32)

    @pl.loop(0, loads)
    def _(g):
        load(g).wait()
        count = jnp.minimum(n - g * GROUP, GROUP)

        @pl.loop(0, (count + UNROLL - 1) // UNROLL)
        def _(u):
            base = g * GROUP + u * UNROLL
            products, targets = [], []
            for i in range(UNROLL):
                b = base + i
                row, col = rows[0, 0, b], cols[0, 0, b]
                if backward:
                    products.append(dot(source[row], held[b]))
                    targets.append(jnp.where(b < n, col, outs))
                else:
                    products.append(dot(held[b], source[col]))
                    targets.append(jnp.where(b < n, row, outs))
            for product, target in zip(products, targets):
                total[target] += product

    if out.dtype == F32:
        @pl.loop(0, outs)
        def _(i):
            out[i] = total[i]
    else:
        @pl.loop(0, outs)
        def _(i):
            out[i] = total[i].astype(out.dtype)


def product_call(rows, cols, live, blocks, source, outs, dtype, backward, name):
    return pl.pallas_call(
        functools.partial(product_kernel, backward),
        out_shape=jax.ShapeDtypeStruct((outs, 128, 128), dtype),
        in_specs=[SM, SM, SM, ANY, VM],
        out_specs=VM,
        scratch_shapes=[
            pltpu.VMEM(blocks.shape, BF16),
            pltpu.VMEM((outs + 1, 128, 128), F32),
            pltpu.SemaphoreType.DMA((blocks.shape[0] // GROUP,)),
        ],
        compiler_params=pltpu.CompilerParams(vmem_limit_bytes=LIMIT),
        name=name,
    )(rows, cols, live, blocks, source)


def sum_row(parts, inbox, total, send, recv, local):
    r, c, z, yl, k = place()
    to, came = row_peers(r)
    copies = [remote(parts.at[p], inbox.at[r], send.at[i], recv.at[i], p, c) for i, p in enumerate(to)]
    for copy in copies:
        copy.start()
    mine = pltpu.make_async_copy(parts.at[r], inbox.at[r], local)
    mine.start()
    mine.wait()
    total[...] = inbox[r].astype(F32)
    order = (6, 4, 5, 1, 2, 3, 0)
    for i in order:
        remote(parts.at[r], inbox.at[came[i]], send.at[i], recv.at[i], to[i], c).wait_recv()
        total[...] += inbox[came[i]].astype(F32)
    return copies


def first_kernel(parts, w_first, b_first, w_second, strip, hidden_t, mask_t, agg_t,
                 inbox, total, outgoing, send, recv, local, gsend, grecv, glocal):
    r, c, z, yl, k = place()
    to, _ = row_peers(r)
    greet([(p, c) for p in to] + [(r, n) for n in col_neighbours(z, yl, k)])
    copies = sum_row(parts, inbox, total, send, recv, local)
    agg = total[...]
    high, low = halves(agg)
    pre = dot(high, w_first[...]) + dot(low, w_first[...]) + b_first[...]
    hidden = jnp.maximum(pre, 0.0).astype(BF16)
    outgoing[...] = dot(hidden, w_second[...]).astype(BF16)
    hidden_t[...] = hidden.astype(F32).T.astype(BF16)
    mask_t[...] = jnp.where(pre > 0, 1.0, 0.0).T.astype(BF16)
    agg_t[...] = agg.T
    gather_col(outgoing, strip, gsend, grecv, glocal)
    for copy in copies:
        copy.wait_send()


def first_call(parts, w_first, b_first, w_second):
    return pl.pallas_call(
        first_kernel,
        out_shape=(
            jax.ShapeDtypeStruct((32, 256, 128), BF16),
            jax.ShapeDtypeStruct((256, 256), BF16),
            jax.ShapeDtypeStruct((256, 256), BF16),
            jax.ShapeDtypeStruct((128, 256), F32),
        ),
        in_specs=[ANY, VM, VM, VM],
        out_specs=(ANY, VM, VM, VM),
        scratch_shapes=[
            pltpu.VMEM((8, 256, 128), F32),
            pltpu.VMEM((256, 128), F32),
            pltpu.VMEM((256, 128), BF16),
            pltpu.SemaphoreType.DMA((7,)),
            pltpu.SemaphoreType.DMA((7,)),
            pltpu.SemaphoreType.DMA,
        ] + GATHER_SCRATCH,
        compiler_params=pltpu.CompilerParams(collective_id=1, has_side_effects=True, vmem_limit_bytes=LIMIT),
        name="first_layer",
    )(parts, w_first, b_first, w_second)


def second_kernel(parts, labels, train, b_second, logits, stats, grads,
                  inbox, total, outgoing, send, recv, local, gsend, grecv, glocal):
    r, c, z, yl, k = place()
    to, came = row_peers(r)
    greet([(p, c) for p in to])
    copies = sum_row(parts, inbox, total, send, recv, local)
    classes = lax.broadcasted_iota(jnp.int32, (128, 256), 0)
    onehot = jnp.where(classes == labels[...], 1.0, 0.0).T
    mask = jnp.broadcast_to(train[...].astype(F32), (128, 256)).T
    scores = total[...] + b_second[...]
    logits[...] = scores.astype(BF16)
    row_max = jnp.max(scores, axis=1, keepdims=True)
    log_total = jnp.log(jnp.sum(jnp.exp(scores - row_max), axis=1, keepdims=True)) + row_max
    count = 32768.0
    d_scores = mask * (jnp.exp(scores - log_total) - onehot) / count
    for half in range(2):
        outgoing[half] = d_scores[128 * half:128 * half + 128].T.astype(BF16)
    sends = [remote(outgoing, grads.at[r], gsend.at[i], grecv.at[i], p, c) for i, p in enumerate(to)]
    for copy in sends:
        copy.start()
    mine = pltpu.make_async_copy(outgoing, grads.at[r], glocal)
    mine.start()
    cross = mask * onehot * (log_total - scores) / count
    stats[...] = jnp.zeros(stats.shape, F32)
    stats[0:1] = jnp.sum(d_scores, axis=0, keepdims=True)
    stats[1:2] = jnp.sum(cross, axis=0, keepdims=True)
    for i in range(7):
        remote(outgoing, grads.at[came[i]], gsend.at[i], grecv.at[i], to[i], c).wait_recv()
    mine.wait()
    for copy in copies + sends:
        copy.wait_send()


def second_call(parts, labels, train, b_second):
    return pl.pallas_call(
        second_kernel,
        out_shape=(
            jax.ShapeDtypeStruct((256, 128), BF16),
            jax.ShapeDtypeStruct((8, 128), F32),
            jax.ShapeDtypeStruct((8, 2, 128, 128), BF16),
        ),
        in_specs=[ANY, VM, VM, VM],
        out_specs=(VM, VM, ANY),
        scratch_shapes=[
            pltpu.VMEM((8, 256, 128), BF16),
            pltpu.VMEM((256, 128), F32),
            pltpu.VMEM((2, 128, 128), BF16),
        ] + 2 * [
            pltpu.SemaphoreType.DMA((7,)),
            pltpu.SemaphoreType.DMA((7,)),
            pltpu.SemaphoreType.DMA,
        ],
        compiler_params=pltpu.CompilerParams(collective_id=2, has_side_effects=True, vmem_limit_bytes=LIMIT),
        name="second_layer",
    )(parts, labels, train, b_second)


STREAMS = ((True, True, 3), (True, False, 4), (False, True, 4), (False, False, 3))
PIECE = 24


def last_kernel(parts, hidden_t, mask_t, agg_t, w_second, stats,
                g_first, g_second, small,
                twin_box, z_out, z_box, y_out, y_box, grad, pay, box_a, box_b, box_c,
                t_send, t_recv, z_send, z_recv, y_send, y_recv,
                a_send, a_recv, b_send, b_recv, c_send, c_recv):
    r, c, z, yl, k = place()
    up, down, across, twin = col_neighbours(z, yl, k)
    me = 4 * r + c % 4

    def of_plane(j):
        return j // 4, 4 * z + j % 4

    def of_line(j):
        return r, 4 * j + c % 4

    barrier = pltpu.get_barrier_semaphore()

    @pl.loop(1, 32)
    def _(i):
        pl.semaphore_signal(barrier, inc=1, device_id=of_plane((me + i) % 32), device_id_type=MESH)

    @pl.loop(1, 8)
    def _(i):
        pl.semaphore_signal(barrier, inc=1, device_id=of_line((z + i) % 8), device_id_type=MESH)

    pl.semaphore_wait(barrier, 38)

    def twin_copy(zz, row):
        i = 2 * zz + row
        return remote(parts.at[4 * zz + 2 * row + 1 - k], twin_box.at[i], t_send.at[i], t_recv.at[i], r, twin)

    def where(other, dz):
        return (z + dz + 8) % 8, (1 - yl if other else yl)

    order = []
    for step in range(4):
        for other, rising, hops in STREAMS:
            if step < hops:
                order.append(where(other, (hops - step) * (1 if rising else -1)))
    order += [where(True, 0), where(False, 0)]
    for zz, row in order:
        twin_copy(zz, row).start()

    def mine(zz, row):
        twin_copy(zz, row).wait_recv()
        return parts[4 * zz + 2 * row + k].astype(F32) + twin_box[2 * zz + row].astype(F32)

    def z_copy(s, step, rising):
        return remote(z_out.at[s, step], z_box.at[s, step], z_send.at[s, step], z_recv.at[s, step], r, up if rising else down)

    for step in range(4):
        for s, (other, rising, hops) in enumerate(STREAMS):
            if step >= hops:
                continue
            zz, row = where(other, (hops - step) * (1 if rising else -1))
            value = mine(zz, row)
            if step:
                z_copy(s, step - 1, rising).wait_recv()
                value += z_box[s, step - 1].astype(F32)
            z_out[s, step] = value.astype(BF16)
            z_copy(s, step, rising).start()
    value = mine(*where(True, 0))
    for s in (0, 1):
        z_copy(s, STREAMS[s][2] - 1, STREAMS[s][1]).wait_recv()
        value += z_box[s, STREAMS[s][2] - 1].astype(F32)
    y_out[...] = value.astype(BF16)
    y_copy = remote(y_out, y_box, y_send, y_recv, r, across)
    y_copy.start()
    value = mine(*where(False, 0))
    for s in (2, 3):
        z_copy(s, STREAMS[s][2] - 1, STREAMS[s][1]).wait_recv()
        value += z_box[s, STREAMS[s][2] - 1].astype(F32)
    y_copy.wait_recv()
    grad[...] = value + y_box[...].astype(F32)

    g_t = jnp.concatenate([grad[0], grad[1]], axis=1)
    g_hi, g_lo = halves(g_t)
    d_pre = (dot(w_second[...], g_hi) + dot(w_second[...], g_lo)) * mask_t[...].astype(F32)
    d_hi, d_lo = halves(d_pre)
    a_hi, a_lo = halves(agg_t[...])
    first = dot_nt(a_hi, d_hi) + dot_nt(a_lo, d_hi) + dot_nt(a_hi, d_lo)
    second = dot_nt(hidden_t[...], g_hi) + dot_nt(hidden_t[...], g_lo)
    ones = jnp.ones((8, 256), BF16)
    bias = dot_nt(ones, d_hi) + dot_nt(ones, d_lo)
    for p in range(8):
        pay[p, 0:16] = first[16 * p:16 * p + 16, 0:128]
        pay[p + 8, 0:16] = first[16 * p:16 * p + 16, 128:256]
    for p in range(16):
        pay[p + 16, 0:16] = second[16 * p:16 * p + 16]
    for p in range(32):
        pay[p, 16:24] = jnp.zeros((8, 128), F32)
    pay[0, 16:24] = stats[...]
    pay[0, 18:19] = bias[0:1, 0:128]
    pay[0, 19:20] = bias[0:1, 128:256]

    def a_copy(to, frm):
        rr, cc = of_plane(to)
        return remote(pay.at[to], box_a.at[frm], a_send.at[to], a_recv.at[frm], rr, cc)

    def b_copy(to, frm):
        rr, cc = of_line(to)
        return remote(box_b.at[z], box_b.at[frm], b_send.at[to], b_recv.at[frm], rr, cc)

    def c_copy(to, frm):
        rr, cc = of_plane(to)
        return remote(box_c.at[me], box_c.at[frm], c_send.at[to], c_recv.at[frm], rr, cc)

    @pl.loop(1, 32)
    def _(i):
        a_copy((me + i) % 32, me).start()

    def add_a(i, total):
        j = (me + 32 - i) % 32
        a_copy(j, j).wait_recv()
        return total + box_a[j]

    box_b[z] = lax.fori_loop(1, 32, add_a, pay[me])

    @pl.loop(1, 8)
    def _(i):
        b_copy((z + i) % 8, z).start()

    @pl.loop(1, 8)
    def _(i):
        j = (z + i) % 8
        b_copy(j, j).wait_recv()

    total = box_b[0]
    for j in range(1, 8):
        total = total + box_b[j]
    box_c[me] = total

    @pl.loop(1, 32)
    def _(i):
        c_copy((me + i) % 32, me).start()

    @pl.loop(1, 32)
    def _(i):
        j = (me + i) % 32
        c_copy(j, j).wait_recv()

    for p in range(8):
        g_first[16 * p:16 * p + 16, 0:128] = box_c[p, 0:16]
        g_first[16 * p:16 * p + 16, 128:256] = box_c[p + 8, 0:16]
    for p in range(16):
        g_second[16 * p:16 * p + 16] = box_c[p + 16, 0:16]
    tail = box_c[0, 16:24]
    lines = lax.broadcasted_iota(jnp.int32, (8, 128), 0)
    whole = jnp.broadcast_to(jnp.sum(tail, axis=1, keepdims=True), (8, 128))
    small[...] = jnp.where(lines == 1, whole, tail)

    for zz, row in order:
        twin_copy(zz, row).wait_send()
    for s, (other, rising, hops) in enumerate(STREAMS):
        for step in range(hops):
            z_copy(s, step, rising).wait_send()
    y_copy.wait_send()

    @pl.loop(1, 32)
    def _(i):
        j = (me + i) % 32
        a_copy(j, me).wait_send()
        c_copy(j, me).wait_send()

    @pl.loop(1, 8)
    def _(i):
        b_copy((z + i) % 8, z).wait_send()


def last_call(parts, hidden_t, mask_t, agg_t, w_second, stats):
    chunk = (2, 128, 128)
    return pl.pallas_call(
        last_kernel,
        out_shape=(
            jax.ShapeDtypeStruct((128, 256), F32),
            jax.ShapeDtypeStruct((256, 128), F32),
            jax.ShapeDtypeStruct((8, 128), F32),
        ),
        in_specs=[VM] * 6,
        out_specs=(VM, VM, VM),
        scratch_shapes=[
            pltpu.VMEM((16,) + chunk, BF16),
            pltpu.VMEM((4, 4) + chunk, BF16),
            pltpu.VMEM((4, 4) + chunk, BF16),
            pltpu.VMEM(chunk, BF16),
            pltpu.VMEM(chunk, BF16),
            pltpu.VMEM(chunk, F32),
            pltpu.VMEM((32, PIECE, 128), F32),
            pltpu.VMEM((32, PIECE, 128), F32),
            pltpu.VMEM((8, PIECE, 128), F32),
            pltpu.VMEM((32, PIECE, 128), F32),
            pltpu.SemaphoreType.DMA((16,)),
            pltpu.SemaphoreType.DMA((16,)),
            pltpu.SemaphoreType.DMA((4, 4)),
            pltpu.SemaphoreType.DMA((4, 4)),
            pltpu.SemaphoreType.DMA,
            pltpu.SemaphoreType.DMA,
            pltpu.SemaphoreType.DMA((32,)),
            pltpu.SemaphoreType.DMA((32,)),
            pltpu.SemaphoreType.DMA((8,)),
            pltpu.SemaphoreType.DMA((8,)),
            pltpu.SemaphoreType.DMA((32,)),
            pltpu.SemaphoreType.DMA((32,)),
        ],
        compiler_params=pltpu.CompilerParams(collective_id=3, has_side_effects=True, vmem_limit_bytes=LIMIT),
        name="weight_gradients",
    )(parts, hidden_t, mask_t, agg_t, w_second, stats)


def local(features, labels, train_mask, adj_rows, adj_cols, adj_live, adj_values, w_first, b_first, w_second, b_second):
    blocks = adj_values[0, 0]
    product = functools.partial(product_call, adj_rows, adj_cols, adj_live, blocks)
    strip = gather_call(features)
    part = product(strip.reshape(64, 128, 128), 16, F32, False, "product_first")
    strip, hidden_t, mask_t, agg_t = first_call(
        part.reshape(8, 256, 128), w_first, b_first.reshape(1, 256), w_second
    )
    part = product(strip.reshape(64, 128, 128), 16, BF16, False, "product_second")
    logits, stats, grads = second_call(
        part.reshape(8, 256, 128), labels.reshape(1, 256), train_mask.reshape(1, 256), b_second.reshape(1, 128)
    )
    part = product(grads.reshape(16, 128, 128), 64, BF16, True, "product_back")
    g_first, g_second, small = last_call(
        part.reshape(32, 2, 128, 128), hidden_t, mask_t, agg_t, w_second, stats
    )
    return logits, small[1, 0], g_first, small[2:4].reshape(256), g_second, small[0]


def solution(mesh):
    in_specs = (
        P(("row", "col"), None),
        P(("row", "col")),
        P(("row", "col")),
        P("row", "col", None),
        P("row", "col", None),
        P("row", "col"),
        P("row", "col", None, None, None),
        P(),
        P(),
        P(),
        P(),
    )
    out_specs = (P(("row", "col"), None), P(), P(), P(), P(), P())
    return jax.shard_map(local, mesh=mesh, in_specs=in_specs, out_specs=out_specs, check_vma=False)
```

time: 944 us -> 158 us (0.17)
  waiting for transfers between devices: 648 us -> 0 us
  Pallas kernels: 0 us -> 149 us
  matrix products: 135 us -> 0 us
  blocking collectives: 80.8 us -> 0 us
  local copies, waits for them, and re-layouts: 49.9 us -> 7.18 us
  between operations: 17.1 us -> 1.49 us
    reduce_scatter x3 -> x0, waiting for transfers between devices: 277 us -> none  [the longest x1 124 us: local(): lax.psum_scatter(tile_backward(blocks, row_ids, col_ids, grad_strip, col_...]
    all_gather x3 -> x0, waiting for transfers between devices: 197 us -> none  [the longest x1 68.8 us: local(): gathered = lax.all_gather(features, 'col', axis=0, tiled=True)]
    psum x1 -> x0, waiting for transfers between devices: 173 us -> none  [local(): lax.psum((grad_w_first, grad_b_first, grad_w_second, grad_b_second), ('ro...]
    pallas_call x0 -> x7, Pallas kernels: none -> 149 us  [the longest x1 46.4 us: last_call(): pl.pallas_call(last_kernel, out_shape=(jax.ShapeDtypeStruct((128, 256), F...]
    dot_general x11 -> x0, matrix products: 135 us -> none  [the longest x2 44.8 us: tile_forward(): summed = jnp.einsum('ik,kaf->iaf', placing, products, precision=highest)]
    psum x1 -> x0, blocking collectives: 80.8 us -> none  [local(): lax.psum(jnp.sum(mask_float * (log_total[:, 0] - picked)), ('row', 'col'))]
    gather x3 -> x0, local copies, waits for them, and re-layouts: 34 us -> none  [the longest x2 20.1 us: tile_forward(): jnp.take(gathered.reshape(-1, block_size, feat_width), col_ids, axis=0)]
    dot_general x3 -> x0, local copies, waits for them, and re-layouts: 11.9 us -> none  [the longest x1 8.08 us: tile_backward(): summed = jnp.einsum('jk,kbf->jbf', placing, products, precision=highest)]
  transfers between devices with their start and end apart: 7 -> 0, of which waited for: 7 -> 0; matrix products, arithmetic and copies ran while one was open for 1% -> 0% of each run, Pallas kernels for 0% -> 0%
where the time goes in v1:
time: 158 us
  Pallas kernels  149 us (94%)
  local copies, waits for them, and re-layouts  7.18 us (5%)
    pallas_call x1, Pallas kernels, last_call(): pl.pallas_call(last_kernel, out_shape=(jax.ShapeDtypeStruct((128, 256), F...  46.4 us
    pallas_call x1, Pallas kernels, first_call(): pl.pallas_call(first_kernel, out_shape=(jax.ShapeDtypeStruct((32, 256, 12...  37 us
    pallas_call x1, Pallas kernels, gather_call(): pl.pallas_call(gather_kernel, out_shape=jax.ShapeDtypeStruct((32,) + feat...  27.1 us
    pallas_call x3, Pallas kernels, product_call(): pl.pallas_call(functools.partial(product_kernel, backward), out_shape=jax...  19.9 us
    pallas_call x1, Pallas kernels, second_call(): pl.pallas_call(second_kernel, out_shape=(jax.ShapeDtypeStruct((256, 128),...  18.9 us
    unnamed x25, local copies, waits for them, and re-layouts  5.59 us

profile of v1, /device:TPU:1, one launch (start us, length us, event | category | flops | bytes accessed | tf_op | source)
XLA Modules:
  0.0 157.9 jit_solution(1982982968778195535)
XLA Ops:
  1.3 0.0 copy-start.3
  1.3 0.8 copy-done.3
  2.2 27.1 %gather_features.1 = bf16[32,256,128]{2,1,0:T(8,128)(2,1)S(1)} custom-call(bf16[256,128]{1,0:T(8,128)(2,1)S(1)} %copy-done.3), custom_call_target="tpu_custom_call" | custom-call | tf_op jit(solution)/shard_map/gather_features/pallas_call | solution.py:124
  29.2 0.0 copy-done.6
  29.2 0.0 copy-done.5
  29.2 0.0 copy-start
  29.3 2.8 %copy-done = bf16[1,1,192,128,128]{4,3,2,1,0:T(8,128)(2,1)S(1)} copy-done((bf16[1,1,192,128,128]{4,3,2,1,0:T(8,128)(2,1)S(1)}, bf16[1,1,192,128,128]{4,3,2,1,0:T(8,128)(2,1)}, u32[]{:S(2)}) %copy-start) | copy-done | bytes 6291480
  32.0 6.6 %product_first.1 = f32[16,128,128]{2,1,0:T(8,128)S(1)} custom-call(s32[1,1,192]{2,1,0:T(1,128)S(1)} %copy-done.5, s32[1,1,192]{2,1,0:T(1,128)S(1)} %copy-done.6, s32[1,1]{1,0:T(1,128)S(6)} %copy.20.live, bf16[192,128,128]{2,1,0:T(8,128)(2,1)S(1)} %bitcast.16, bf16[64,128,128]{2,1,0:T(8,128)(2,1)S(1)} %bitcast.20), custom_call_target="tpu_custom_call" | custom-call | tf_op jit(solution)/shard_map/product_first/pallas_call | solution.py:185
  38.6 0.0 copy-done.2
  38.6 0.0 copy-done.4
  38.7 37.0 %first_layer.1 = (bf16[32,256,128]{2,1,0:T(8,128)(2,1)S(1)}, bf16[256,256]{1,0:T(8,128)(2,1)S(1)}, bf16[256,256]{1,0:T(8,128)(2,1)S(1)}, f32[128,256]{1,0:T(8,128)S(1)}) custom-call(f32[8,256,128]{2,1,0:T(8,128)S(1)} %bitcast.21, bf16[128,256]{1,0:T(8,128)(2,1)S(1)} %copy-done.4, f32[1,256]{1,0:T(1,128)S(1)} %bitcast.27, bf16[256,128]{1,0:T(8,128)(2,1)S(1)} %copy-done.2), custom_call_target="tpu_custom_call" | custom-call | tf_op jit(solution)/shard_map/first_layer/pallas_call | solution.py:237
  75.7 0.0 copy-start.7
  75.7 0.0 copy-start.8
  75.7 0.0 copy-start.10
  75.7 6.5 %product_second.1 = bf16[16,128,128]{2,1,0:T(8,128)(2,1)S(1)} custom-call(s32[1,1,192]{2,1,0:T(1,128)S(1)} %copy-done.5, s32[1,1,192]{2,1,0:T(1,128)S(1)} %copy-done.6, s32[1,1]{1,0:T(1,128)S(6)} %copy.20.live, bf16[192,128,128]{2,1,0:T(8,128)(2,1)S(1)} %bitcast.17, bf16[64,128,128]{2,1,0:T(8,128)(2,1)S(1)} %bitcast.22), custom_call_target="tpu_custom_call" | custom-call | tf_op jit(solution)/shard_map/product_second/pallas_call | solution.py:185
  82.2 18.9 %second_layer.1 = (bf16[256,128]{1,0:T(8,128)(2,1)S(1)}, f32[8,128]{1,0:T(8,128)S(1)}, bf16[8,2,128,128]{3,2,1,0:T(8,128)(2,1)S(1)}) custom-call(bf16[8,256,128]{2,1,0:T(8,128)(2,1)S(1)} %bitcast.23, s32[1,256]{1,0:T(1,128)S(1)} %bitcast.25, s32[1,256]{1,0:T(1,128)S(1)} %bitcast.26, f32[1,128]{1,0:T(1,128)S(1)} %bitcast.28), custom_call_target="tpu_custom_call" | custom-call | tf_op jit(solution)/shard_map/second_layer/pallas_call | solution.py:294
  101.1 6.9 %product_back.1 = bf16[64,128,128]{2,1,0:T(8,128)(2,1)S(1)} custom-call(s32[1,1,192]{2,1,0:T(1,128)S(1)} %copy-done.5, s32[1,1,192]{2,1,0:T(1,128)S(1)} %copy-done.6, s32[1,1]{1,0:T(1,128)S(6)} %copy.20.live, bf16[192,128,128]{2,1,0:T(8,128)(2,1)S(1)} %bitcast.18, bf16[16,128,128]{2,1,0:T(8,128)(2,1)S(1)} %bitcast.24), custom_call_target="tpu_custom_call" | custom-call | tf_op jit(solution)/shard_map/product_back/pallas_call | solution.py:185
  108.0 46.4 %weight_gradients.1 = (f32[128,256]{1,0:T(8,128)S(1)}, f32[256,128]{1,0:T(8,128)S(1)}, f32[8,128]{1,0:T(8,128)S(1)}) custom-call(bf16[32,2,128,128]{3,2,1,0:T(8,128)(2,1)S(1)} %bitcast.19, bf16[256,256]{1,0:T(8,128)(2,1)S(1)} %get-tuple-element.19.hidden_t, bf16[256,256]{1,0:T(8,128)(2,1)S(1)} %get-tuple-element.20.mask_t, ...), custom_call_target="tpu_custom_call" | custom-call | tf_op jit(solution)/shard_map/weight_gradients/pallas_call | solution.py:492
  154.4 0.5 slice.9
  154.9 0.5 slice_bitcast_fusion.1
  155.4 0.6 slice_bitcast_fusion
  156.0 0.6 copy.21
  156.6 0.7 copy.22
  157.3 0.7 copy.23
  (11 shorter events, 0.0 us)
Async XLA Ops:
  0.6 28.6 %copy-start.6 = (s32[1,1,192]{2,1,0:T(1,128)S(1)}, s32[1,1,192]{2,1,0:T(1,128)}, u32[]{:S(2)}) copy-start(s32[1,1,192]{2,1,0:T(1,128)} %cols.5) | copy-start | bytes 2308
  0.6 28.6 %copy-start.5 = (s32[1,1,192]{2,1,0:T(1,128)S(1)}, s32[1,1,192]{2,1,0:T(1,128)}, u32[]{:S(2)}) copy-start(s32[1,1,192]{2,1,0:T(1,128)} %rows.5) | copy-start | bytes 2308
  1.3 0.8 copy-start.3
  29.2 2.8 %copy-start = (bf16[1,1,192,128,128]{4,3,2,1,0:T(8,128)(2,1)S(1)}, bf16[1,1,192,128,128]{4,3,2,1,0:T(8,128)(2,1)}, u32[]{:S(2)}) copy-start(bf16[1,1,192,128,128]{4,3,2,1,0:T(8,128)(2,1)} %param.17) | copy-start | bytes 18874372
  32.0 6.6 %copy-start.2 = (bf16[256,128]{1,0:T(8,128)(2,1)S(1)}, bf16[256,128]{1,0:T(8,128)(2,1)}, u32[]{:S(2)}) copy-start(bf16[256,128]{1,0:T(8,128)(2,1)} %w_second.3) | copy-start | bytes 196612
  32.0 6.6 %copy-start.4 = (bf16[128,256]{1,0:T(8,128)(2,1)S(1)}, bf16[128,256]{1,0:T(8,128)(2,1)}, u32[]{:S(2)}) copy-start(bf16[128,256]{1,0:T(8,128)(2,1)} %w_first.1) | copy-start | bytes 196612
  32.0 6.6 %copy-start.9 = (f32[256]{0:T(256)S(1)}, f32[256]{0:T(256)}, u32[]{:S(2)}) copy-start(f32[256]{0:T(256)} %param.19) | copy-start | bytes 3076
  32.0 43.6 %copy-start.1 = (bf16[1,1,192,128,128]{4,3,2,1,0:T(8,128)(2,1)S(1)}, bf16[1,1,192,128,128]{4,3,2,1,0:T(8,128)(2,1)}, u32[]{:S(2)}) copy-start(bf16[1,1,192,128,128]{4,3,2,1,0:T(8,128)(2,1)} %param.17) | copy-start | bytes 18874372
  75.7 6.5 %copy-start.7 = (s32[256]{0:T(256)S(1)}, s32[256]{0:T(256)}, u32[]{:S(2)}) copy-start(s32[256]{0:T(256)} %param.12) | copy-start | bytes 3076
  75.7 6.5 %copy-start.8 = (s32[256]{0:T(256)S(1)}, s32[256]{0:T(256)}, u32[]{:S(2)}) copy-start(s32[256]{0:T(256)} %param.13) | copy-start | bytes 3076
  75.7 6.5 %copy-start.10 = (f32[128]{0:T(128)S(1)}, f32[128]{0:T(128)}, u32[]{:S(2)}) copy-start(f32[128]{0:T(128)} %param.21) | copy-start | bytes 1540

commit v2 on v1

v2 whole, which is shorter than its diff:
```python
import functools

import jax
import jax.numpy as jnp
from jax import lax
from jax.experimental import pallas as pl
from jax.experimental.pallas import tpu as pltpu
from jax.sharding import PartitionSpec as P

MESH = pl.DeviceIdType.MESH
F32, BF16 = jnp.float32, jnp.bfloat16
ANY = pl.BlockSpec(memory_space=pl.ANY)
VM = pl.BlockSpec(memory_space=pltpu.VMEM)
SM = pl.BlockSpec(memory_space=pltpu.SMEM)
LIMIT = 32 * 1024 * 1024
PRODUCT_LIMIT = 12 * 1024 * 1024
UNROLL = 32
LOADS = 4


def dot(a, b):
    return jnp.dot(a, b, preferred_element_type=F32)


def dot_nt(a, b):
    return lax.dot_general(a, b, (((1,), (1,)), ((), ())), preferred_element_type=F32)


def halves(a):
    hi = a.astype(BF16)
    return hi, (a - hi.astype(F32)).astype(BF16)


def place():
    r, c = lax.axis_index("row"), lax.axis_index("col")
    return r, c, c // 4, (c // 2) % 2, c % 2


def remote(src, dst, send, recv, r, c):
    return pltpu.make_async_remote_copy(
        src_ref=src, dst_ref=dst, send_sem=send, recv_sem=recv,
        device_id=(r, c), device_id_type=MESH,
    )


def col_neighbours(z, yl, k):
    up, down = (z + 1) % 8, (z + 7) % 8
    return (4 * up + 2 * yl + k, 4 * down + 2 * yl + k, 4 * z + 2 * (1 - yl) + k, 4 * z + 2 * yl + 1 - k)


def row_peers(r):
    x, yh = r % 4, r // 4
    to, came = [], []
    for dy, dx in ((1, 2), (0, 2), (1, 1), (1, 3), (0, 1), (0, 3), (1, 0)):
        y2 = (yh + dy) % 2
        to.append(4 * y2 + (x + dx) % 4)
        came.append(4 * y2 + (x + 4 - dx) % 4)
    return to, came


def greet(devices):
    barrier = pltpu.get_barrier_semaphore()
    for device in devices:
        pl.semaphore_signal(barrier, inc=1, device_id=device, device_id_type=MESH)
    pl.semaphore_wait(barrier, len(devices))


def gather_scratch(pieces):
    return [
        pltpu.SemaphoreType.DMA((36 * pieces,)),
        pltpu.SemaphoreType.DMA((32, pieces)),
        pltpu.SemaphoreType.DMA((pieces,)),
    ]


class Gather:
    STAGES = (
        ((-1, False, "ut"), (1, False, "dt"), (0, True, "udt")),
        ((-2, False, "uat"), (2, False, "dt"), (1, True, "dt"), (-1, True, "t")),
        ((-3, False, "uat"), (3, False, "at"), (2, True, "t"), (-2, True, "t")),
        ((-4, False, "at"), (-3, True, "t"), (3, True, "t")),
        ((-4, True, "t"),),
    )

    def __init__(self, src, out, pieces, send, recv, local):
        self.src, self.out, self.pieces, self.send, self.recv, self.local = src, out, pieces, send, recv, local
        self.rows = src.shape[0] // pieces
        self.r, self.c, self.z, self.yl, self.k = place()
        up, down, across, twin = col_neighbours(self.z, self.yl, self.k)
        self.to = {"u": up, "d": down, "a": across, "t": twin}
        self.started, self.kept = [], []

    def slot(self, dz, other):
        return 4 * ((self.z + dz + 8) % 8) + 2 * (1 - self.yl if other else self.yl) + self.k

    def part(self, slot, s):
        return self.out.at[slot, pl.ds(s * self.rows, self.rows)]

    def push(self, block, slot, s, targets):
        for name in targets:
            copy = remote(block, self.part(slot, s), self.send.at[len(self.started)], self.recv.at[slot, s], self.r, self.to[name])
            copy.start()
            self.started.append(copy)

    def arrived(self, slot, s):
        block = self.part(slot, s)
        remote(block, block, self.send.at[0], self.recv.at[slot, s], self.r, self.to["t"]).wait_recv()

    def begin(self, s):
        block = self.src.at[pl.ds(s * self.rows, self.rows)]
        self.push(block, self.c, s, "udat")
        mine = pltpu.make_async_copy(block, self.part(self.c, s), self.local.at[s])
        mine.start()
        self.kept.append(mine)

    def stage(self, n, s):
        for dz, other, targets in self.STAGES[n - 1]:
            slot = self.slot(dz, other)
            self.arrived(slot, s)
            self.push(self.part(slot, s), slot, s, targets)

    def end(self):
        for s in range(self.pieces):
            for dz in range(8):
                for other in (False, True):
                    self.arrived(self.slot(dz, other) + 1 - 2 * self.k, s)
        for copy in self.kept:
            copy.wait()
        for copy in self.started:
            copy.wait_send()


def gather_kernel(src, blocks, out, held, load_sem, *sems):
    r, c, z, yl, k = place()
    greet([(r, n) for n in col_neighbours(z, yl, k)])
    gather = Gather(src, out, 1, *sems)
    gather.begin(0)
    share = blocks.shape[0] // LOADS
    loads = [
        pltpu.make_async_copy(blocks.at[pl.ds(i * share, share)], held.at[pl.ds(i * share, share)], load_sem.at[i])
        for i in range(LOADS)
    ]
    for load in loads:
        load.start()
    for n in range(1, 6):
        gather.stage(n, 0)
    gather.end()
    for load in loads:
        load.wait()


def gather_call(features, blocks):
    return pl.pallas_call(
        gather_kernel,
        out_shape=(
            jax.ShapeDtypeStruct((32,) + features.shape, BF16),
            jax.ShapeDtypeStruct(blocks.shape, BF16),
        ),
        in_specs=[ANY, ANY],
        out_specs=(VM, VM),
        scratch_shapes=[pltpu.SemaphoreType.DMA((LOADS,))] + gather_scratch(1),
        compiler_params=pltpu.CompilerParams(collective_id=0, has_side_effects=True, vmem_limit_bytes=LIMIT),
        name="gather_features",
    )(pltpu.with_memory_space_constraint(features, pltpu.HBM), pltpu.with_memory_space_constraint(blocks, pltpu.HBM))


def product_kernel(backward, rows, cols, live, blocks, source, out, total):
    n = live[0, 0]
    outs = total.shape[0] - 1

    @pl.loop(0, outs, unroll=2)
    def _(i):
        total[i] = jnp.zeros(total.shape[1:], F32)

    @pl.loop(0, (n + UNROLL - 1) // UNROLL)
    def _(u):
        products, targets = [], []
        for i in range(UNROLL):
            b = u * UNROLL + i
            row, col = rows[0, 0, b], cols[0, 0, b]
            if backward:
                products.append(dot(source[row], blocks[b]))
                targets.append(jnp.where(b < n, col, outs))
            else:
                products.append(dot(blocks[b], source[col]))
                targets.append(jnp.where(b < n, row, outs))
        for product, target in zip(products, targets):
            total[target] += product

    @pl.loop(0, outs, unroll=2)
    def _(i):
        out[i] = total[i].astype(out.dtype)


def product_call(rows, cols, live, blocks, source, outs, dtype, backward, name):
    return pl.pallas_call(
        functools.partial(product_kernel, backward),
        out_shape=jax.ShapeDtypeStruct((outs, 128, 128), dtype),
        in_specs=[SM, SM, SM, VM, VM],
        out_specs=VM,
        scratch_shapes=[pltpu.VMEM((outs + 1, 128, 128), F32)],
        compiler_params=pltpu.CompilerParams(vmem_limit_bytes=PRODUCT_LIMIT),
        name=name,
    )(rows, cols, live, blocks, source)


class RowSum:
    def __init__(self, parts, inbox, pieces, send, recv, local):
        self.parts, self.inbox, self.send, self.recv, self.local = parts, inbox, send, recv, local
        self.rows = inbox.shape[1] // pieces
        self.r, self.c, _, _, _ = place()
        self.to, self.came = row_peers(self.r)
        self.copies, self.mine = [], []
        for s in range(pieces):
            for i in range(7):
                self.copies.append(self.copy(i, self.r, s))
                self.copies[-1].start()
            part = pl.ds(s * self.rows, self.rows)
            self.mine.append(pltpu.make_async_copy(parts.at[self.r, part], inbox.at[self.r, part], local.at[s]))
            self.mine[-1].start()

    def copy(self, i, slot, s):
        part = pl.ds(s * self.rows, self.rows)
        return remote(self.parts.at[self.to[i], part], self.inbox.at[slot, part], self.send.at[i, s], self.recv.at[i, s], self.to[i], self.c)

    def piece(self, s):
        part = slice(s * self.rows, (s + 1) * self.rows)
        self.mine[s].wait()
        total = self.inbox[self.r, part].astype(F32)
        for i in (6, 4, 5, 1, 2, 3, 0):
            self.copy(i, self.came[i], s).wait_recv()
            total = total + self.inbox[self.came[i], part].astype(F32)
        return total

    def end(self):
        for copy in self.copies:
            copy.wait_send()


def first_kernel(parts, w_first, b_first, w_second, strip, hidden_t, mask_t, agg_t,
                 inbox, outgoing, send, recv, local, gsend, grecv, glocal):
    r, c, z, yl, k = place()
    to, _ = row_peers(r)
    greet([(p, c) for p in to] + [(r, n) for n in col_neighbours(z, yl, k)])
    row_sum = RowSum(parts, inbox, 1, send, recv, local)
    gather = Gather(outgoing, strip, 1, gsend, grecv, glocal)

    def begin(s):
        agg = row_sum.piece(s)
        high, low = halves(agg)
        pre = dot(high, w_first[...]) + dot(low, w_first[...]) + b_first[...]
        hidden = jnp.maximum(pre, 0.0).astype(BF16)
        part = slice(0, 256)
        outgoing[part] = dot(hidden, w_second[...]).astype(BF16)
        gather.begin(s)
        hidden_t[:, part] = hidden.astype(F32).T.astype(BF16)
        mask_t[:, part] = jnp.where(pre > 0, 1.0, 0.0).T.astype(BF16)
        agg_t[:, part] = agg.T

    begin(0)
    for n in range(1, 6):
        gather.stage(n, 0)
    gather.end()
    row_sum.end()


def first_call(parts, w_first, b_first, w_second):
    return pl.pallas_call(
        first_kernel,
        out_shape=(
            jax.ShapeDtypeStruct((32, 256, 128), BF16),
            jax.ShapeDtypeStruct((256, 256), BF16),
            jax.ShapeDtypeStruct((256, 256), BF16),
            jax.ShapeDtypeStruct((128, 256), F32),
        ),
        in_specs=[ANY, VM, VM, VM],
        out_specs=(VM, VM, VM, VM),
        scratch_shapes=[
            pltpu.VMEM((8, 256, 128), F32),
            pltpu.VMEM((256, 128), BF16),
            pltpu.SemaphoreType.DMA((7, 2)),
            pltpu.SemaphoreType.DMA((7, 2)),
            pltpu.SemaphoreType.DMA((2,)),
        ] + gather_scratch(2),
        compiler_params=pltpu.CompilerParams(collective_id=1, has_side_effects=True, vmem_limit_bytes=LIMIT),
        name="first_layer",
    )(parts, w_first, b_first, w_second)


def second_kernel(parts, labels, train, b_second, logits, stats, grads,
                  inbox, outgoing, send, recv, local, gsend, grecv, glocal):
    r, c, z, yl, k = place()
    to, came = row_peers(r)
    greet([(p, c) for p in to])
    row_sum = RowSum(parts, inbox, 2, send, recv, local)
    classes = lax.broadcasted_iota(jnp.int32, (128, 256), 0)
    onehot = jnp.where(classes == labels[...], 1.0, 0.0).T
    mask = jnp.broadcast_to(train[...].astype(F32), (128, 256)).T
    count = 32768.0
    sends, mine = [], []
    stats[...] = jnp.zeros(stats.shape, F32)

    def grad_copy(i, slot, s):
        return remote(outgoing.at[s], grads.at[slot, s], gsend.at[i, s], grecv.at[i, s], to[i], c)

    for s in range(2):
        part = slice(128 * s, 128 * s + 128)
        scores = row_sum.piece(s) + b_second[...]
        row_max = jnp.max(scores, axis=1, keepdims=True)
        log_total = jnp.log(jnp.sum(jnp.exp(scores - row_max), axis=1, keepdims=True)) + row_max
        d_scores = mask[part] * (jnp.exp(scores - log_total) - onehot[part]) / count
        outgoing[s] = d_scores.T.astype(BF16)
        for i in range(7):
            sends.append(grad_copy(i, r, s))
            sends[-1].start()
        mine.append(pltpu.make_async_copy(outgoing.at[s], grads.at[r, s], glocal.at[s]))
        mine[-1].start()
        logits[part] = scores.astype(BF16)
        cross = mask[part] * onehot[part] * (log_total - scores) / count
        stats[0:1] += jnp.sum(d_scores, axis=0, keepdims=True)
        stats[1:2] += jnp.sum(cross, axis=0, keepdims=True)
    for s in range(2):
        for i in range(7):
            grad_copy(i, came[i], s).wait_recv()
        mine[s].wait()
    row_sum.end()
    for copy in sends:
        copy.wait_send()


def second_call(parts, labels, train, b_second):
    return pl.pallas_call(
        second_kernel,
        out_shape=(
            jax.ShapeDtypeStruct((256, 128), BF16),
            jax.ShapeDtypeStruct((8, 128), F32),
            jax.ShapeDtypeStruct((8, 2, 128, 128), BF16),
        ),
        in_specs=[ANY, VM, VM, VM],
        out_specs=(VM, VM, VM),
        scratch_shapes=[
            pltpu.VMEM((8, 256, 128), BF16),
            pltpu.VMEM((2, 128, 128), BF16),
        ] + 2 * [
            pltpu.SemaphoreType.DMA((7, 2)),
            pltpu.SemaphoreType.DMA((7, 2)),
            pltpu.SemaphoreType.DMA((2,)),
        ],
        compiler_params=pltpu.CompilerParams(collective_id=2, has_side_effects=True, vmem_limit_bytes=LIMIT),
        name="second_layer",
    )(parts, labels, train, b_second)


STREAMS = ((True, True, 3), (True, False, 4), (False, True, 4), (False, False, 3))
PIECE = 24


def last_kernel(parts, hidden_t, mask_t, agg_t, w_second, stats,
                sums,
                twin_box, z_out, z_box, y_out, y_box, grad, pay, box_t, half, box_x, quarter, box_y, box_z,
                t_send, t_recv, z_send, z_recv, y_send, y_recv,
                a_send, a_recv, b_send, b_recv, c_send, c_recv):
    r, c, z, yl, k = place()
    up, down, across, twin = col_neighbours(z, yl, k)
    x, y = r % 4, 2 * (r // 4) + yl

    def on_x(j):
        return r - x + j, c

    def on_y(j):
        return 4 * (j // 2) + x, 4 * z + 2 * (j % 2) + k

    def on_z(j):
        return r, 4 * j + 2 * yl + k

    greet([on_x((x + i) % 4) for i in (1, 2, 3)] + [on_y((y + i) % 4) for i in (1, 2, 3)]
          + [on_z((z + i) % 8) for i in range(1, 8)] + [(r, twin)])

    def twin_copy(zz, row):
        i = 2 * zz + row
        return remote(parts.at[4 * zz + 2 * row + 1 - k], twin_box.at[i], t_send.at[i], t_recv.at[i], r, twin)

    def where(other, dz):
        return (z + dz + 8) % 8, (1 - yl if other else yl)

    order = []
    for step in range(4):
        for other, rising, hops in STREAMS:
            if step < hops:
                order.append(where(other, (hops - step) * (1 if rising else -1)))
    order += [where(True, 0), where(False, 0)]
    for zz, row in order:
        twin_copy(zz, row).start()

    def mine(zz, row):
        twin_copy(zz, row).wait_recv()
        return parts[4 * zz + 2 * row + k].astype(F32) + twin_box[2 * zz + row].astype(F32)

    def z_copy(s, step, rising):
        return remote(z_out.at[s, step], z_box.at[s, step], z_send.at[s, step], z_recv.at[s, step], r, up if rising else down)

    for step in range(4):
        for s, (other, rising, hops) in enumerate(STREAMS):
            if step >= hops:
                continue
            zz, row = where(other, (hops - step) * (1 if rising else -1))
            value = mine(zz, row)
            if step:
                z_copy(s, step - 1, rising).wait_recv()
                value += z_box[s, step - 1].astype(F32)
            z_out[s, step] = value.astype(BF16)
            z_copy(s, step, rising).start()
    value = mine(*where(True, 0))
    for s in (0, 1):
        z_copy(s, STREAMS[s][2] - 1, STREAMS[s][1]).wait_recv()
        value += z_box[s, STREAMS[s][2] - 1].astype(F32)
    y_out[...] = value.astype(BF16)
    y_copy = remote(y_out, y_box, y_send, y_recv, r, across)
    y_copy.start()
    value = mine(*where(False, 0))
    for s in (2, 3):
        z_copy(s, STREAMS[s][2] - 1, STREAMS[s][1]).wait_recv()
        value += z_box[s, STREAMS[s][2] - 1].astype(F32)
    y_copy.wait_recv()
    grad[...] = value + y_box[...].astype(F32)

    g_t = jnp.concatenate([grad[0], grad[1]], axis=1)
    g_hi, g_lo = halves(g_t)
    d_pre = (dot(w_second[...], g_hi) + dot(w_second[...], g_lo)) * mask_t[...].astype(F32)
    d_hi, d_lo = halves(d_pre)
    a_hi, a_lo = halves(agg_t[...])
    first = dot_nt(a_hi, d_hi) + dot_nt(a_lo, d_hi) + dot_nt(a_hi, d_lo)
    second = dot_nt(hidden_t[...], g_hi) + dot_nt(hidden_t[...], g_lo)
    ones = jnp.ones((8, 256), BF16)
    bias = dot_nt(ones, d_hi) + dot_nt(ones, d_lo)
    for p in range(8):
        pay[p, 0:16] = first[16 * p:16 * p + 16, 0:128]
        pay[p + 8, 0:16] = first[16 * p:16 * p + 16, 128:256]
    for p in range(16):
        pay[p + 16, 0:16] = second[16 * p:16 * p + 16]
    for p in range(32):
        pay[p, 16:24] = jnp.zeros((8, 128), F32)
    pay[0, 16:24] = stats[...]
    pay[0, 18:19] = bias[0:1, 0:128]
    pay[0, 19:20] = bias[0:1, 128:256]

    mine16, mine4, p = 16 * k, 16 * k + 4 * x, 16 * k + 4 * x + y
    half_copy = remote(pay.at[pl.ds(16 - mine16, 16)], box_t, a_send.at[0], a_recv.at[0], r, twin)
    half_copy.start()
    half_copy.wait_recv()
    half[...] = pay[pl.ds(mine16, 16)] + box_t[...]

    def x_copy(j, frm):
        return remote(half.at[pl.ds(4 * j, 4)], box_x.at[frm], b_send.at[0, j], b_recv.at[0, frm], *on_x(j))

    def y_part(j, frm):
        return remote(quarter.at[j], box_y.at[frm], b_send.at[1, j], b_recv.at[1, frm], *on_y(j))

    def z_part(j, frm):
        return remote(box_z.at[z], box_z.at[frm], c_send.at[j], c_recv.at[frm], *on_z(j))

    def y_back(j, frm):
        block = sums.at[mine4 + frm]
        return remote(block, block, b_send.at[2, j], b_recv.at[2, frm], *on_y(j))

    def x_back(j, frm):
        block = sums.at[pl.ds(mine16 + 4 * frm, 4)]
        return remote(block, block, b_send.at[3, j], b_recv.at[3, frm], *on_x(j))

    xs, ys, zs = [(x + i) % 4 for i in (2, 1, 3)], [(y + i) % 4 for i in (2, 1, 3)], [(z + i) % 8 for i in (4, 3, 5, 2, 6, 1, 7)]

    def exchange(copy, peers, me):
        for j in peers:
            copy(j, me).start()
        for j in reversed(peers):
            copy(j, j).wait_recv()

    exchange(x_copy, xs, x)
    total = half[pl.ds(4 * x, 4)]
    for j in xs:
        total = total + box_x[j]
    quarter[...] = total
    exchange(y_part, ys, y)
    total = quarter[y]
    for j in ys:
        total = total + box_y[j]
    box_z[z] = total
    exchange(z_part, zs, z)
    total = box_z[0]
    for j in range(1, 8):
        total = total + box_z[j]
    sums[p] = total
    exchange(y_back, ys, y)
    exchange(x_back, xs, x)
    back = sums.at[pl.ds(mine16, 16)]
    back_copy = remote(back, back, a_send.at[1], a_recv.at[1], r, twin)
    back_copy.start()
    other_half = sums.at[pl.ds(16 - mine16, 16)]
    remote(other_half, other_half, a_send.at[1], a_recv.at[1], r, twin).wait_recv()

    for zz, row in order:
        twin_copy(zz, row).wait_send()
    for s, (other, rising, hops) in enumerate(STREAMS):
        for step in range(hops):
            z_copy(s, step, rising).wait_send()
    y_copy.wait_send()
    half_copy.wait_send()
    back_copy.wait_send()
    for copy, peers, me in ((x_copy, xs, x), (y_part, ys, y), (z_part, zs, z), (y_back, ys, y), (x_back, xs, x)):
        for j in peers:
            copy(j, me).wait_send()


def last_call(parts, hidden_t, mask_t, agg_t, w_second, stats):
    chunk = (2, 128, 128)
    return pl.pallas_call(
        last_kernel,
        out_shape=jax.ShapeDtypeStruct((32, PIECE, 128), F32),
        in_specs=[VM] * 6,
        out_specs=VM,
        scratch_shapes=[
            pltpu.VMEM((16,) + chunk, BF16),
            pltpu.VMEM((4, 4) + chunk, BF16),
            pltpu.VMEM((4, 4) + chunk, BF16),
            pltpu.VMEM(chunk, BF16),
            pltpu.VMEM(chunk, BF16),
            pltpu.VMEM(chunk, F32),
            pltpu.VMEM((32, PIECE, 128), F32),
            pltpu.VMEM((16, PIECE, 128), F32),
            pltpu.VMEM((16, PIECE, 128), F32),
            pltpu.VMEM((4, 4, PIECE, 128), F32),
            pltpu.VMEM((4, PIECE, 128), F32),
            pltpu.VMEM((4, PIECE, 128), F32),
            pltpu.VMEM((8, PIECE, 128), F32),
            pltpu.SemaphoreType.DMA((16,)),
            pltpu.SemaphoreType.DMA((16,)),
            pltpu.SemaphoreType.DMA((4, 4)),
            pltpu.SemaphoreType.DMA((4, 4)),
            pltpu.SemaphoreType.DMA,
            pltpu.SemaphoreType.DMA,
            pltpu.SemaphoreType.DMA((2,)),
            pltpu.SemaphoreType.DMA((2,)),
            pltpu.SemaphoreType.DMA((4, 4)),
            pltpu.SemaphoreType.DMA((4, 4)),
            pltpu.SemaphoreType.DMA((8,)),
            pltpu.SemaphoreType.DMA((8,)),
        ],
        compiler_params=pltpu.CompilerParams(collective_id=3, has_side_effects=True, vmem_limit_bytes=LIMIT),
        name="weight_gradients",
    )(parts, hidden_t, mask_t, agg_t, w_second, stats)


def finish_kernel(sums, scores, logits, loss, g_first, b_first, g_second, b_second):
    logits[...] = scores[...]
    for p in range(8):
        g_first[16 * p:16 * p + 16, 0:128] = sums[p, 0:16]
        g_first[16 * p:16 * p + 16, 128:256] = sums[p + 8, 0:16]
    for p in range(16):
        g_second[16 * p:16 * p + 16] = sums[p + 16, 0:16]
    b_second[...] = sums[0, 16:17]
    loss[...] = jnp.sum(sums[0, 17:18], axis=1, keepdims=True)
    b_first[:, 0:128] = sums[0, 18:19]
    b_first[:, 128:256] = sums[0, 19:20]


def finish_call(sums, scores):
    return pl.pallas_call(
        finish_kernel,
        out_shape=(
            jax.ShapeDtypeStruct((256, 128), BF16),
            jax.ShapeDtypeStruct((1, 1), F32),
            jax.ShapeDtypeStruct((128, 256), F32),
            jax.ShapeDtypeStruct((1, 256), F32),
            jax.ShapeDtypeStruct((256, 128), F32),
            jax.ShapeDtypeStruct((1, 128), F32),
        ),
        in_specs=[VM, VM],
        out_specs=(VM,) * 6,
        compiler_params=pltpu.CompilerParams(vmem_limit_bytes=4 * 1024 * 1024),
        name="outputs",
    )(sums, scores)


def local(features, labels, train_mask, adj_rows, adj_cols, adj_live, adj_values, w_first, b_first, w_second, b_second):
    strip, blocks = gather_call(features, adj_values[0, 0])
    product = functools.partial(product_call, adj_rows, adj_cols, adj_live, blocks)
    part = product(strip.reshape(64, 128, 128), 16, F32, False, "product_first")
    strip, hidden_t, mask_t, agg_t = first_call(
        part.reshape(8, 256, 128), w_first, b_first.reshape(1, 256), w_second
    )
    part = product(strip.reshape(64, 128, 128), 16, BF16, False, "product_second")
    scores, stats, grads = second_call(
        part.reshape(8, 256, 128), labels.reshape(1, 256), train_mask.reshape(1, 256), b_second.reshape(1, 128)
    )
    part = product(grads.reshape(16, 128, 128), 64, BF16, True, "product_back")
    sums = last_call(part.reshape(32, 2, 128, 128), hidden_t, mask_t, agg_t, w_second, stats)
    logits, loss, g_first, gb_first, g_second, gb_second = finish_call(sums, scores)
    return logits, loss.reshape(()), g_first, gb_first.reshape(256), g_second, gb_second.reshape(128)


def solution(mesh):
    in_specs = (
        P(("row", "col"), None),
        P(("row", "col")),
        P(("row", "col")),
        P("row", "col", None),
        P("row", "col", None),
        P("row", "col"),
        P("row", "col", None, None, None),
        P(),
        P(),
        P(),
        P(),
    )
    out_specs = (P(("row", "col"), None), P(), P(), P(), P(), P())
    return jax.shard_map(local, mesh=mesh, in_specs=in_specs, out_specs=out_specs, check_vma=False)
```

time: 158 us -> 142 us (0.90)
  Pallas kernels: 149 us -> 140 us
  local copies, waits for them, and re-layouts: 7.18 us -> 0.05 us
    pallas_call x3, Pallas kernels: 19.9 us -> 9.95 us  [product_call(): pl.pallas_call(functools.partial(product_kernel, backward), out_shape=jax...]
    unnamed x25 -> x16, local copies, waits for them, and re-layouts: 5.59 us -> 0.05 us
    pallas_call x1, Pallas kernels: 37 us -> 39.3 us  [first_call(): pl.pallas_call(first_kernel, out_shape=(jax.ShapeDtypeStruct((32, 256, 12...]
    pallas_call x1, Pallas kernels: 18.9 us -> 17.1 us  [second_call(): pl.pallas_call(second_kernel, out_shape=(jax.ShapeDtypeStruct((256, 128),...]
    pallas_call x2 -> x3, Pallas kernels: 73.5 us -> 73.7 us  [the longest x1 46.9 us: last_call(): pl.pallas_call(last_kernel, out_shape=jax.ShapeDtypeStruct((32, PIECE, 12...]
where the time goes in v2:
time: 142 us
  Pallas kernels  140 us (99%)
  between operations  1.46 us (1%)
    pallas_call x1, Pallas kernels, last_call(): pl.pallas_call(last_kernel, out_shape=jax.ShapeDtypeStruct((32, PIECE, 12...  46.9 us
    pallas_call x1, Pallas kernels, first_call(): pl.pallas_call(first_kernel, out_shape=(jax.ShapeDtypeStruct((32, 256, 12...  39.3 us
    pallas_call x1, Pallas kernels, gather_call(): pl.pallas_call(gather_kernel, out_shape=(jax.ShapeDtypeStruct((32,) + fea...  26 us
    pallas_call x1, Pallas kernels, second_call(): pl.pallas_call(second_kernel, out_shape=(jax.ShapeDtypeStruct((256, 128),...  17.1 us
    pallas_call x3, Pallas kernels, product_call(): pl.pallas_call(functools.partial(product_kernel, backward), out_shape=jax...  9.95 us

profile of v2, /device:TPU:1, one launch (start us, length us, event | category | flops | bytes accessed | tf_op | source)
XLA Modules:
  0.0 141.6 jit_solution(9038821925745293841)
XLA Ops:
  1.3 0.0 copy-start.2
  1.3 0.0 copy-start.3
  1.3 26.0 %gather_features.1 = (bf16[32,256,128]{2,1,0:T(8,128)(2,1)S(1)}, bf16[192,128,128]{2,1,0:T(8,128)(2,1)S(1)}) custom-call(bf16[256,128]{1,0:T(8,128)(2,1)} %src.1, bf16[192,128,128]{2,1,0:T(8,128)(2,1)} %bitcast.24), custom_call_target="tpu_custom_call" | custom-call | tf_op jit(solution)/shard_map/gather_features/pallas_call | solution.py:153
  27.3 0.0 copy-done.2
  27.3 0.0 copy-done.3
  27.4 0.0 copy-start
  27.4 0.0 copy-start.1
  27.4 0.0 copy-start.6
  27.4 3.1 %product_first.1 = f32[16,128,128]{2,1,0:T(8,128)S(1)} custom-call(s32[1,1,192]{2,1,0:T(1,128)S(1)} %copy-done.2, s32[1,1,192]{2,1,0:T(1,128)S(1)} %copy-done.3, s32[1,1]{1,0:T(1,128)S(6)} %copy.17.live, bf16[192,128,128]{2,1,0:T(8,128)(2,1)S(1)} %get-tuple-element.21.blocks, bf16[64,128,128]{2,1,0:T(8,128)(2,1)S(1)} %bitcast.18), custom_call_target="tpu_custom_call" | custom-call | tf_op jit(solution)/shard_map/product_first/pallas_call | solution.py:196
  30.5 0.0 copy-done
  30.6 0.0 copy-done.1
  30.6 0.0 copy-done.6
  30.6 39.3 %first_layer.1 = (bf16[32,256,128]{2,1,0:T(8,128)(2,1)S(1)}, bf16[256,256]{1,0:T(8,128)(2,1)S(1)}, bf16[256,256]{1,0:T(8,128)(2,1)S(1)}, f32[128,256]{1,0:T(8,128)S(1)}) custom-call(f32[8,256,128]{2,1,0:T(8,128)S(1)} %bitcast.15, bf16[128,256]{1,0:T(8,128)(2,1)S(1)} %copy-done.1, f32[1,256]{1,0:T(1,128)S(1)} %bitcast.22, bf16[256,128]{1,0:T(8,128)(2,1)S(1)} %copy-done), custom_call_target="tpu_custom_call" | custom-call | tf_op jit(solution)/shard_map/first_layer/pallas_call | solution.py:268
  69.9 0.0 copy-start.4
  69.9 0.0 copy-start.5
  69.9 0.0 copy-start.7
  70.0 3.1 %product_second.1 = bf16[16,128,128]{2,1,0:T(8,128)(2,1)S(1)} custom-call(s32[1,1,192]{2,1,0:T(1,128)S(1)} %copy-done.2, s32[1,1,192]{2,1,0:T(1,128)S(1)} %copy-done.3, s32[1,1]{1,0:T(1,128)S(6)} %copy.17.live, bf16[192,128,128]{2,1,0:T(8,128)(2,1)S(1)} %get-tuple-element.21.blocks, bf16[64,128,128]{2,1,0:T(8,128)(2,1)S(1)} %bitcast.16), custom_call_target="tpu_custom_call" | custom-call | tf_op jit(solution)/shard_map/product_second/pallas_call | solution.py:196
  73.1 0.0 copy-done.4
  73.1 0.0 copy-done.5
  73.1 0.0 copy-done.7
  73.1 17.1 %second_layer.1 = (bf16[256,128]{1,0:T(8,128)(2,1)S(1)}, f32[8,128]{1,0:T(8,128)S(1)}, bf16[8,2,128,128]{3,2,1,0:T(8,128)(2,1)S(1)}) custom-call(bf16[8,256,128]{2,1,0:T(8,128)(2,1)S(1)} %bitcast.17, s32[1,256]{1,0:T(1,128)S(1)} %bitcast.20, s32[1,256]{1,0:T(1,128)S(1)} %bitcast.21, f32[1,128]{1,0:T(1,128)S(1)} %bitcast.23), custom_call_target="tpu_custom_call" | custom-call | tf_op jit(solution)/shard_map/second_layer/pallas_call | solution.py:332
  90.2 3.7 %product_back.1 = bf16[64,128,128]{2,1,0:T(8,128)(2,1)S(1)} custom-call(s32[1,1,192]{2,1,0:T(1,128)S(1)} %copy-done.2, s32[1,1,192]{2,1,0:T(1,128)S(1)} %copy-done.3, s32[1,1]{1,0:T(1,128)S(6)} %copy.17.live, bf16[192,128,128]{2,1,0:T(8,128)(2,1)S(1)} %get-tuple-element.21.blocks, bf16[16,128,128]{2,1,0:T(8,128)(2,1)S(1)} %bitcast.19), custom_call_target="tpu_custom_call" | custom-call | tf_op jit(solution)/shard_map/product_back/pallas_call | solution.py:196
  93.9 46.9 %weight_gradients.1.sums = f32[32,24,128]{2,1,0:T(8,128)S(1)} custom-call(bf16[32,2,128,128]{3,2,1,0:T(8,128)(2,1)S(1)} %bitcast.14, bf16[256,256]{1,0:T(8,128)(2,1)S(1)} %get-tuple-element.25.hidden_t, bf16[256,256]{1,0:T(8,128)(2,1)S(1)} %get-tuple-element.26.mask_t, f32[128,256]{1,0:T(8,128)S(1)} %get-tuple-element.27.agg_t, ...), custom_call_target="tpu_custom_call" | custom-call | tf_op jit(solution)/shard_map/weight_gradients/pallas_call | solution.py:516
  140.8 0.7 outputs.1
Async XLA Ops:
  1.3 26.1 %copy-start.2 = (s32[1,1,192]{2,1,0:T(1,128)S(1)}, s32[1,1,192]{2,1,0:T(1,128)}, u32[]{:S(2)}) copy-start(s32[1,1,192]{2,1,0:T(1,128)} %rows.5) | copy-start | bytes 2308
  1.3 26.1 %copy-start.3 = (s32[1,1,192]{2,1,0:T(1,128)S(1)}, s32[1,1,192]{2,1,0:T(1,128)}, u32[]{:S(2)}) copy-start(s32[1,1,192]{2,1,0:T(1,128)} %cols.5) | copy-start | bytes 2308
  27.4 3.2 %copy-start = (bf16[256,128]{1,0:T(8,128)(2,1)S(1)}, bf16[256,128]{1,0:T(8,128)(2,1)}, u32[]{:S(2)}) copy-start(bf16[256,128]{1,0:T(8,128)(2,1)} %w_second.3) | copy-start | bytes 196612
  27.4 3.2 %copy-start.1 = (bf16[128,256]{1,0:T(8,128)(2,1)S(1)}, bf16[128,256]{1,0:T(8,128)(2,1)}, u32[]{:S(2)}) copy-start(bf16[128,256]{1,0:T(8,128)(2,1)} %w_first.1) | copy-start | bytes 196612
  27.4 3.2 %copy-start.6 = (f32[256]{0:T(256)S(1)}, f32[256]{0:T(256)}, u32[]{:S(2)}) copy-start(f32[256]{0:T(256)} %param.19) | copy-start | bytes 3076
  69.9 3.2 %copy-start.4 = (s32[256]{0:T(256)S(1)}, s32[256]{0:T(256)}, u32[]{:S(2)}) copy-start(s32[256]{0:T(256)} %param.12) | copy-start | bytes 3076
  69.9 3.2 %copy-start.5 = (s32[256]{0:T(256)S(1)}, s32[256]{0:T(256)}, u32[]{:S(2)}) copy-start(s32[256]{0:T(256)} %param.13) | copy-start | bytes 3076
  69.9 3.2 %copy-start.7 = (f32[128]{0:T(128)S(1)}, f32[128]{0:T(128)}, u32[]{:S(2)}) copy-start(f32[128]{0:T(128)} %param.21) | copy-start | bytes 1540

commit v3 on v2

v3 whole, which is shorter than its diff:
```python
import functools

import jax
import jax.numpy as jnp
from jax import lax
from jax.experimental import pallas as pl
from jax.experimental.pallas import tpu as pltpu
from jax.sharding import PartitionSpec as P

MESH = pl.DeviceIdType.MESH
F32, BF16 = jnp.float32, jnp.bfloat16
ANY = pl.BlockSpec(memory_space=pl.ANY)
VM = pl.BlockSpec(memory_space=pltpu.VMEM)
SM = pl.BlockSpec(memory_space=pltpu.SMEM)
LIMIT = 32 * 1024 * 1024
PRODUCT_LIMIT = 24 * 1024 * 1024
UNROLL = 32
STEP = 2048
PIECES, STAGGER = 2, False
ORDER = tuple((n, s) for n in range(6) for s in range(2))
LOADS = 4


def dot(a, b):
    return jnp.dot(a, b, preferred_element_type=F32)


def dot_tn(a, b):
    return lax.dot_general(a, b, (((0,), (0,)), ((), ())), preferred_element_type=F32)


def halves(a):
    hi = a.astype(BF16)
    return hi, (a - hi.astype(F32)).astype(BF16)


def place():
    r, c = lax.axis_index("row"), lax.axis_index("col")
    return r, c, c // 4, (c // 2) % 2, c % 2


def remote(src, dst, send, recv, r, c):
    return pltpu.make_async_remote_copy(
        src_ref=src, dst_ref=dst, send_sem=send, recv_sem=recv,
        device_id=(r, c), device_id_type=MESH,
    )


def col_neighbours(z, yl, k):
    up, down = (z + 1) % 8, (z + 7) % 8
    return (4 * up + 2 * yl + k, 4 * down + 2 * yl + k, 4 * z + 2 * (1 - yl) + k, 4 * z + 2 * yl + 1 - k)


def row_peers(r):
    x, yh = r % 4, r // 4
    to, came = [], []
    for dy, dx in ((1, 2), (0, 2), (1, 1), (1, 3), (0, 1), (0, 3), (1, 0)):
        y2 = (yh + dy) % 2
        to.append(4 * y2 + (x + dx) % 4)
        came.append(4 * y2 + (x + 4 - dx) % 4)
    return to, came


def greet(devices):
    barrier = pltpu.get_barrier_semaphore()
    for device in devices:
        pl.semaphore_signal(barrier, inc=1, device_id=device, device_id_type=MESH)
    pl.semaphore_wait(barrier, len(devices))


def gather_scratch(pieces):
    return [
        pltpu.SemaphoreType.DMA((36 * pieces,)),
        pltpu.SemaphoreType.DMA((32, pieces)),
        pltpu.SemaphoreType.DMA((pieces,)),
    ]


class Gather:
    STAGES = (
        ((-1, False, "ut"), (1, False, "dt"), (0, True, "udt")),
        ((-2, False, "uat"), (2, False, "dt"), (1, True, "dt"), (-1, True, "t")),
        ((-3, False, "uat"), (3, False, "at"), (2, True, "t"), (-2, True, "t")),
        ((-4, False, "at"), (-3, True, "t"), (3, True, "t")),
        ((-4, True, "t"),),
    )

    def __init__(self, src, out, pieces, send, recv, local):
        self.src, self.out, self.pieces, self.send, self.recv, self.local = src, out, pieces, send, recv, local
        self.rows = src.shape[0] // pieces
        self.r, self.c, self.z, self.yl, self.k = place()
        up, down, across, twin = col_neighbours(self.z, self.yl, self.k)
        self.to = {"u": up, "d": down, "a": across, "t": twin}
        self.started, self.kept = [], []

    def slot(self, dz, other):
        return 4 * ((self.z + dz + 8) % 8) + 2 * (1 - self.yl if other else self.yl) + self.k

    def part(self, slot, s):
        return self.out.at[slot, pl.ds(s * self.rows, self.rows)]

    def push(self, block, slot, s, targets):
        for name in targets:
            copy = remote(block, self.part(slot, s), self.send.at[len(self.started)], self.recv.at[slot, s], self.r, self.to[name])
            copy.start()
            self.started.append(copy)

    def arrived(self, slot, s):
        block = self.part(slot, s)
        remote(block, block, self.send.at[0], self.recv.at[slot, s], self.r, self.to["t"]).wait_recv()

    def begin(self, s):
        block = self.src.at[pl.ds(s * self.rows, self.rows)]
        self.push(block, self.c, s, "udat")
        mine = pltpu.make_async_copy(block, self.part(self.c, s), self.local.at[s])
        mine.start()
        self.kept.append(mine)

    def stage(self, n, s):
        for dz, other, targets in self.STAGES[n - 1]:
            slot = self.slot(dz, other)
            self.arrived(slot, s)
            self.push(self.part(slot, s), slot, s, targets)

    def end(self):
        for s in range(self.pieces):
            for dz in range(8):
                for other in (False, True):
                    self.arrived(self.slot(dz, other) + 1 - 2 * self.k, s)
        for copy in self.kept:
            copy.wait()
        for copy in self.started:
            copy.wait_send()


def gather_kernel(src, blocks, out, held, load_sem, *sems):
    r, c, z, yl, k = place()
    greet([(r, n) for n in col_neighbours(z, yl, k)])
    gather = Gather(src, out, 1, *sems)
    gather.begin(0)
    share = blocks.shape[0] // LOADS
    loads = [
        pltpu.make_async_copy(blocks.at[pl.ds(i * share, share)], held.at[pl.ds(i * share, share)], load_sem.at[i])
        for i in range(LOADS)
    ]
    for load in loads:
        load.start()
    for n in range(1, 6):
        gather.stage(n, 0)
    gather.end()
    for load in loads:
        load.wait()


def gather_call(features, blocks):
    return pl.pallas_call(
        gather_kernel,
        out_shape=(
            jax.ShapeDtypeStruct((32,) + features.shape, BF16),
            jax.ShapeDtypeStruct(blocks.shape, BF16),
        ),
        in_specs=[ANY, ANY],
        out_specs=(VM, VM),
        scratch_shapes=[pltpu.SemaphoreType.DMA((LOADS,))] + gather_scratch(1),
        compiler_params=pltpu.CompilerParams(collective_id=0, has_side_effects=True, vmem_limit_bytes=LIMIT),
        name="gather_features",
    )(pltpu.with_memory_space_constraint(features, pltpu.HBM), pltpu.with_memory_space_constraint(blocks, pltpu.HBM))


def sparse_product(backward, rows, cols, live, blocks, source, total):
    n = jnp.max(live[...])
    outs = total.shape[0] - 1

    @pl.loop(0, outs, unroll=2)
    def _(i):
        total[i] = jnp.zeros(total.shape[1:], F32)

    @pl.loop(0, (n + UNROLL - 1) // UNROLL)
    def _(u):
        products, targets = [], []
        for i in range(UNROLL):
            b = u * UNROLL + i
            row, col = rows[0, 0, b], cols[0, 0, b]
            if backward:
                products.append(dot_tn(blocks[b], source[row]))
                targets.append(jnp.where(b < n, col, outs))
            else:
                products.append(dot(blocks[b], source[col]))
                targets.append(jnp.where(b < n, row, outs))
        for product, target in zip(products, targets):
            total[target] += product


def product_first_kernel(rows, cols, live, blocks, source, out, total):
    sparse_product(False, rows, cols, live, blocks, source, total)

    @pl.loop(0, out.shape[0], unroll=2)
    def _(i):
        out[i] = total[i]


def product_second_kernel(rows, cols, live, blocks, agg, w_first, b_first, w_second, out, hidden, source, total):
    nodes = STEP // 128

    @pl.loop(0, source.shape[0] // nodes)
    def _(i):
        part = pl.ds(i * nodes, nodes)
        high, low = halves(agg[part].reshape(STEP, 128))
        pre = dot(high, w_first[...]) + dot(low, w_first[...]) + b_first[...]
        kept = jnp.maximum(pre, 0.0).astype(BF16)
        hidden[part] = kept.reshape(nodes, 128, 256)
        source[part] = dot(kept, w_second[...]).astype(BF16).reshape(nodes, 128, 128)

    sparse_product(False, rows, cols, live, blocks, source, total)

    @pl.loop(0, out.shape[0], unroll=2)
    def _(i):
        out[i] = total[i].astype(BF16)


def product_back_kernel(rows, cols, live, blocks, source, agg, hidden, w_second, stats, pay,
                        total, g_first, g_second, g_bias):
    sparse_product(True, rows, cols, live, blocks, source, total)
    nodes = STEP // 128
    w_second_t = w_second[...].astype(F32).T.astype(BF16)
    g_first[...] = jnp.zeros(g_first.shape, F32)
    g_second[...] = jnp.zeros(g_second.shape, F32)
    g_bias[...] = jnp.zeros(g_bias.shape, F32)

    @pl.loop(0, hidden.shape[0] // nodes)
    def _(i):
        part = pl.ds(i * nodes, nodes)
        grad = total[part].reshape(STEP, 128).astype(BF16)
        kept = hidden[part].reshape(STEP, 256)
        d_pre = jnp.where(kept > 0, dot(grad, w_second_t), 0.0)
        g_second[...] += dot_tn(kept, grad)
        g_first[...] += dot_tn(agg[part].reshape(STEP, 128).astype(BF16), d_pre.astype(BF16))
        g_bias[...] += jnp.sum(d_pre.reshape(STEP // 8, 8, 256), axis=0)

    for p in range(8):
        pay[p, 0:16] = g_first[16 * p:16 * p + 16, 0:128]
        pay[p + 8, 0:16] = g_first[16 * p:16 * p + 16, 128:256]
    for p in range(16):
        pay[p + 16, 0:16] = g_second[16 * p:16 * p + 16]
    for p in range(4, 32):
        pay[p, 16:17] = jnp.zeros((1, 128), F32)
    bias = jnp.sum(g_bias[...], axis=0, keepdims=True)
    pay[0, 16:17] = stats[0:1]
    pay[1, 16:17] = stats[1:2]
    pay[2, 16:17] = bias[:, 0:128]
    pay[3, 16:17] = bias[:, 128:256]


def product_call(kernel, index, dense, out_shape, outs, scratch, name):
    return pl.pallas_call(
        kernel,
        out_shape=out_shape,
        in_specs=[SM, SM] + [VM] * (2 + len(dense)),
        out_specs=jax.tree.map(lambda _: VM, out_shape),
        scratch_shapes=scratch + [pltpu.VMEM((outs + 1, 128, 128), F32)] if name != "product_back"
        else [pltpu.VMEM((outs + 1, 128, 128), F32)] + scratch,
        compiler_params=pltpu.CompilerParams(vmem_limit_bytes=PRODUCT_LIMIT),
        name=name,
    )(*index, *dense)


class RowSum:
    def __init__(self, parts, inbox, pieces, send, recv, local):
        self.parts, self.inbox, self.send, self.recv, self.local = parts, inbox, send, recv, local
        self.rows = inbox.shape[1] // pieces
        self.r, self.c, _, _, _ = place()
        self.to, self.came = row_peers(self.r)
        self.copies, self.mine = [], []
        for s in range(pieces):
            if s and STAGGER:
                for copy in self.copies:
                    copy.wait_send()
            for i in range(7):
                self.copies.append(self.copy(i, self.r, s))
                self.copies[-1].start()
            part = pl.ds(s * self.rows, self.rows)
            self.mine.append(pltpu.make_async_copy(parts.at[self.r, part], inbox.at[self.r, part], local.at[s]))
            self.mine[-1].start()
        self.waiting = self.copies[7 * (pieces - 1):] if STAGGER else self.copies

    def copy(self, i, slot, s):
        part = pl.ds(s * self.rows, self.rows)
        return remote(self.parts.at[self.to[i], part], self.inbox.at[slot, part], self.send.at[i, s], self.recv.at[i, s], self.to[i], self.c)

    def piece(self, s):
        part = slice(s * self.rows, (s + 1) * self.rows)
        self.mine[s].wait()
        total = self.inbox[self.r, part].astype(F32)
        for i in (6, 4, 5, 1, 2, 3, 0):
            self.copy(i, self.came[i], s).wait_recv()
            total = total + self.inbox[self.came[i], part].astype(F32)
        return total

    def end(self):
        for copy in self.waiting:
            copy.wait_send()


def first_kernel(parts, strip, inbox, outgoing, send, recv, local, gsend, grecv, glocal):
    r, c, z, yl, k = place()
    to, _ = row_peers(r)
    greet([(p, c) for p in to] + [(r, n) for n in col_neighbours(z, yl, k)])
    row_sum = RowSum(parts, inbox, PIECES, send, recv, local)
    gather = Gather(outgoing, strip, PIECES, gsend, grecv, glocal)
    for n, s in ORDER:
        if n == 0:
            outgoing[gather.rows * s:gather.rows * (s + 1)] = row_sum.piece(s)
            gather.begin(s)
        else:
            gather.stage(n, s)
    gather.end()
    row_sum.end()


def first_call(parts):
    return pl.pallas_call(
        first_kernel,
        out_shape=jax.ShapeDtypeStruct((32, 256, 128), F32),
        in_specs=[ANY],
        out_specs=VM,
        scratch_shapes=[
            pltpu.VMEM((8, 256, 128), F32),
            pltpu.VMEM((256, 128), F32),
            pltpu.SemaphoreType.DMA((7, PIECES)),
            pltpu.SemaphoreType.DMA((7, PIECES)),
            pltpu.SemaphoreType.DMA((PIECES,)),
        ] + gather_scratch(PIECES),
        compiler_params=pltpu.CompilerParams(collective_id=1, has_side_effects=True, vmem_limit_bytes=LIMIT),
        name="first_layer",
    )(parts)


def second_kernel(parts, labels, train, b_second, logits, stats, grads,
                  inbox, outgoing, send, recv, local, gsend, grecv, glocal):
    r, c, z, yl, k = place()
    to, came = row_peers(r)
    greet([(p, c) for p in to])
    row_sum = RowSum(parts, inbox, 2, send, recv, local)
    classes = lax.broadcasted_iota(jnp.int32, (128, 256), 0)
    onehot = jnp.where(classes == labels[...], 1.0, 0.0).T
    mask = jnp.broadcast_to(train[...].astype(F32), (128, 256)).T
    count = 32768.0
    sends, mine = [], []
    stats[...] = jnp.zeros(stats.shape, F32)

    def grad_copy(i, slot, s):
        return remote(outgoing.at[s], grads.at[slot, s], gsend.at[i, s], grecv.at[i, s], to[i], c)

    for s in range(2):
        part = slice(128 * s, 128 * s + 128)
        scores = row_sum.piece(s) + b_second[...]
        row_max = jnp.max(scores, axis=1, keepdims=True)
        log_total = jnp.log(jnp.sum(jnp.exp(scores - row_max), axis=1, keepdims=True)) + row_max
        d_scores = mask[part] * (jnp.exp(scores - log_total) - onehot[part]) / count
        outgoing[s] = d_scores.astype(BF16)
        for i in range(7):
            sends.append(grad_copy(i, r, s))
            sends[-1].start()
        mine.append(pltpu.make_async_copy(outgoing.at[s], grads.at[r, s], glocal.at[s]))
        mine[-1].start()
        logits[part] = scores.astype(BF16)
        cross = mask[part] * onehot[part] * (log_total - scores) / count
        stats[0:1] += jnp.sum(d_scores, axis=0, keepdims=True)
        stats[1:2] += jnp.sum(cross, axis=0, keepdims=True)
    for s in range(2):
        for i in range(7):
            grad_copy(i, came[i], s).wait_recv()
        mine[s].wait()
    row_sum.end()
    for copy in sends:
        copy.wait_send()


def second_call(parts, labels, train, b_second):
    return pl.pallas_call(
        second_kernel,
        out_shape=(
            jax.ShapeDtypeStruct((256, 128), BF16),
            jax.ShapeDtypeStruct((8, 128), F32),
            jax.ShapeDtypeStruct((8, 2, 128, 128), BF16),
        ),
        in_specs=[ANY, VM, VM, VM],
        out_specs=(VM, VM, VM),
        scratch_shapes=[
            pltpu.VMEM((8, 256, 128), BF16),
            pltpu.VMEM((2, 128, 128), BF16),
        ] + 2 * [
            pltpu.SemaphoreType.DMA((7, 2)),
            pltpu.SemaphoreType.DMA((7, 2)),
            pltpu.SemaphoreType.DMA((2,)),
        ],
        compiler_params=pltpu.CompilerParams(collective_id=2, has_side_effects=True, vmem_limit_bytes=LIMIT),
        name="second_layer",
    )(parts, labels, train, b_second)


PIECE = 17


def last_kernel(pay, sums, box_t, half, box_p, box_z, t_send, t_recv, p_send, p_recv, z_send, z_recv):
    r, c, z, yl, k = place()
    me, mine16 = 4 * (r % 4) + 2 * (r // 4) + yl, 16 * k

    def on_plane(j):
        return 4 * (j % 4 // 2) + j // 4, 4 * z + 2 * (j % 2) + k

    def on_z(j):
        return r, 4 * j + 2 * yl + k

    def others(n, first, then):
        @pl.loop(1, n)
        def _(i):
            then(lax.rem(first + i, n))

    barrier = pltpu.get_barrier_semaphore()

    def signal(device):
        pl.semaphore_signal(barrier, inc=1, device_id=device, device_id_type=MESH)

    others(8, z, lambda j: signal(on_z(j)))
    others(16, me, lambda j: signal(on_plane(j)))
    twin = (r, 4 * z + 2 * yl + 1 - k)
    signal(twin)
    pl.semaphore_wait(barrier, 23)

    half_copy = remote(pay.at[pl.ds(16 - mine16, 16)], box_t, t_send.at[0], t_recv.at[0], *twin)
    half_copy.start()
    half_copy.wait_recv()
    half[...] = pay[pl.ds(mine16, 16)] + box_t[...]

    def plane_copy(j, frm):
        return remote(half.at[j], box_p.at[frm], p_send.at[0, j], p_recv.at[0, frm], *on_plane(j))

    def z_copy(j, frm):
        return remote(box_z.at[z], box_z.at[frm], z_send.at[j], z_recv.at[frm], *on_z(j))

    def plane_back(j, frm):
        block = sums.at[mine16 + frm]
        return remote(block, block, p_send.at[1, j], p_recv.at[1, frm], *on_plane(j))

    others(16, me, lambda j: plane_copy(j, me).start())
    box_p[me] = half[me]
    others(16, me, lambda j: plane_copy(j, j).wait_recv())
    total = box_p[0]
    for j in range(1, 16):
        total = total + box_p[j]
    box_z[z] = total
    others(8, z, lambda j: z_copy(j, z).start())
    others(8, z, lambda j: z_copy(j, j).wait_recv())
    total = box_z[0]
    for j in range(1, 8):
        total = total + box_z[j]
    sums[mine16 + me] = total
    others(16, me, lambda j: plane_back(j, me).start())
    others(16, me, lambda j: plane_back(j, j).wait_recv())
    back = sums.at[pl.ds(mine16, 16)]
    back_copy = remote(back, back, t_send.at[1], t_recv.at[1], *twin)
    back_copy.start()
    other_half = sums.at[pl.ds(16 - mine16, 16)]
    remote(other_half, other_half, t_send.at[1], t_recv.at[1], *twin).wait_recv()
    half_copy.wait_send()
    back_copy.wait_send()
    others(8, z, lambda j: z_copy(j, z).wait_send())
    others(16, me, lambda j: plane_copy(j, me).wait_send())
    others(16, me, lambda j: plane_back(j, me).wait_send())


def last_call(pay):
    return pl.pallas_call(
        last_kernel,
        out_shape=jax.ShapeDtypeStruct((32, PIECE, 128), F32),
        in_specs=[VM],
        out_specs=VM,
        scratch_shapes=[
            pltpu.VMEM((16, PIECE, 128), F32),
            pltpu.VMEM((16, PIECE, 128), F32),
            pltpu.VMEM((16, PIECE, 128), F32),
            pltpu.VMEM((8, PIECE, 128), F32),
            pltpu.SemaphoreType.DMA((2,)),
            pltpu.SemaphoreType.DMA((2,)),
            pltpu.SemaphoreType.DMA((2, 16)),
            pltpu.SemaphoreType.DMA((2, 16)),
            pltpu.SemaphoreType.DMA((8,)),
            pltpu.SemaphoreType.DMA((8,)),
        ],
        compiler_params=pltpu.CompilerParams(collective_id=3, has_side_effects=True, vmem_limit_bytes=LIMIT),
        name="weight_gradients",
    )(pay)


def finish_kernel(sums, scores, logits, loss, g_first, b_first, g_second, b_second):
    logits[...] = scores[...]
    for p in range(8):
        g_first[16 * p:16 * p + 16, 0:128] = sums[p, 0:16]
        g_first[16 * p:16 * p + 16, 128:256] = sums[p + 8, 0:16]
    for p in range(16):
        g_second[16 * p:16 * p + 16] = sums[p + 16, 0:16]
    b_second[...] = sums[0, 16:17]
    loss[...] = jnp.sum(sums[1, 16:17], axis=1, keepdims=True)
    b_first[:, 0:128] = sums[2, 16:17]
    b_first[:, 128:256] = sums[3, 16:17]


def finish_call(sums, scores):
    return pl.pallas_call(
        finish_kernel,
        out_shape=(
            jax.ShapeDtypeStruct((256, 128), BF16),
            jax.ShapeDtypeStruct((1, 1), F32),
            jax.ShapeDtypeStruct((128, 256), F32),
            jax.ShapeDtypeStruct((1, 256), F32),
            jax.ShapeDtypeStruct((256, 128), F32),
            jax.ShapeDtypeStruct((1, 128), F32),
        ),
        in_specs=[VM, VM],
        out_specs=(VM,) * 6,
        compiler_params=pltpu.CompilerParams(vmem_limit_bytes=4 * 1024 * 1024),
        name="outputs",
    )(sums, scores)


def local(features, labels, train_mask, adj_rows, adj_cols, adj_live, adj_values, w_first, b_first, w_second, b_second):
    strip, blocks = gather_call(features, adj_values[0, 0])
    index = (adj_rows, adj_cols, adj_live, blocks)
    shape = jax.ShapeDtypeStruct
    part = product_call(
        product_first_kernel, index, (strip.reshape(64, 128, 128),), shape((16, 128, 128), F32), 16, [], "product_first"
    )
    agg = first_call(part.reshape(8, 256, 128)).reshape(64, 128, 128)
    part, hidden = product_call(
        product_second_kernel, index, (agg, w_first, b_first.reshape(1, 256), w_second),
        (shape((16, 128, 128), BF16), shape((64, 128, 256), BF16)), 16, [pltpu.VMEM((64, 128, 128), BF16)], "product_second",
    )
    scores, stats, grads = second_call(
        part.reshape(8, 256, 128), labels.reshape(1, 256), train_mask.reshape(1, 256), b_second.reshape(1, 128)
    )
    pay = product_call(
        product_back_kernel, index, (grads.reshape(16, 128, 128), agg, hidden, w_second, stats),
        shape((32, PIECE, 128), F32), 64,
        [pltpu.VMEM((128, 256), F32), pltpu.VMEM((256, 128), F32), pltpu.VMEM((8, 256), F32)], "product_back",
    )
    sums = last_call(pay)
    logits, loss, g_first, gb_first, g_second, gb_second = finish_call(sums, scores)
    return logits, loss.reshape(()), g_first, gb_first.reshape(256), g_second, gb_second.reshape(128)


def solution(mesh):
    in_specs = (
        P(("row", "col"), None),
        P(("row", "col")),
        P(("row", "col")),
        P("row", "col", None),
        P("row", "col", None),
        P("row", "col"),
        P("row", "col", None, None, None),
        P(),
        P(),
        P(),
        P(),
    )
    out_specs = (P(("row", "col"), None), P(), P(), P(), P(), P())
    return jax.shard_map(local, mesh=mesh, in_specs=in_specs, out_specs=out_specs, check_vma=False)
```

time: 142 us -> 128 us (0.901)
  Pallas kernels: 140 us -> 127 us
    pallas_call x1, Pallas kernels: 46.9 us -> 23.3 us  [last_call(): pl.pallas_call(last_kernel, out_shape=jax.ShapeDtypeStruct((32, PIECE, 12...]
    pallas_call x4, Pallas kernels: 49.3 us -> 58.1 us  [the longest x1 43.7 us: first_call(): pl.pallas_call(first_kernel, out_shape=jax.ShapeDtypeStruct((32, 256, 128...]
    pallas_call x1, Pallas kernels: 17.1 us -> 18.7 us  [second_call(): pl.pallas_call(second_kernel, out_shape=(jax.ShapeDtypeStruct((256, 128),...]
where the time goes in v3:
time: 128 us
  Pallas kernels  127 us (99%)
  between operations  1.48 us (1%)
    pallas_call x1, Pallas kernels, first_call(): pl.pallas_call(first_kernel, out_shape=jax.ShapeDtypeStruct((32, 256, 128...  43.7 us
    pallas_call x1, Pallas kernels, gather_call(): pl.pallas_call(gather_kernel, out_shape=(jax.ShapeDtypeStruct((32,) + fea...  26 us
    pallas_call x1, Pallas kernels, last_call(): pl.pallas_call(last_kernel, out_shape=jax.ShapeDtypeStruct((32, PIECE, 12...  23.3 us
    pallas_call x1, Pallas kernels, second_call(): pl.pallas_call(second_kernel, out_shape=(jax.ShapeDtypeStruct((256, 128),...  18.7 us
    pallas_call x3, Pallas kernels, product_call(): pl.pallas_call(kernel, out_shape=out_shape, in_specs=[SM, SM] + [VM] * (2...  14.3 us

profile of v3, /device:TPU:1, one launch (start us, length us, event | category | flops | bytes accessed | tf_op | source)
XLA Modules:
  0.0 128.4 jit_solution(8767194998544437164)
XLA Ops:
  0.6 0.0 copy-start.3
  0.6 0.0 copy-start.2
  1.3 26.0 %gather_features.1 = (bf16[32,256,128]{2,1,0:T(8,128)(2,1)S(1)}, bf16[192,128,128]{2,1,0:T(8,128)(2,1)S(1)}) custom-call(bf16[256,128]{1,0:T(8,128)(2,1)} %src.1, bf16[192,128,128]{2,1,0:T(8,128)(2,1)} %bitcast.23), custom_call_target="tpu_custom_call" | custom-call | tf_op jit(solution)/shard_map/gather_features/pallas_call | solution.py:156
  27.4 0.0 copy-done.3
  27.4 0.0 copy-done.2
  27.4 1.8 %product_first.1 = f32[16,128,128]{2,1,0:T(8,128)S(1)} custom-call(s32[1,1,192]{2,1,0:T(1,128)S(1)} %copy-done.2, s32[1,1,192]{2,1,0:T(1,128)S(1)} %copy-done.3, s32[1,1]{1,0:T(1,128)S(6)} %copy.17.live, bf16[192,128,128]{2,1,0:T(8,128)(2,1)S(1)} %get-tuple-element.19.blocks, bf16[64,128,128]{2,1,0:T(8,128)(2,1)S(1)} %bitcast.16), custom_call_target="tpu_custom_call" | custom-call | tf_op jit(solution)/shard_map/product_first/pallas_call | solution.py:255
  29.1 0.0 copy-start
  29.1 0.0 copy-start.1
  29.2 0.0 copy-start.4
  29.2 43.7 %first_layer.1 = f32[32,256,128]{2,1,0:T(8,128)S(1)} custom-call(f32[8,256,128]{2,1,0:T(8,128)S(1)} %bitcast.15), custom_call_target="tpu_custom_call" | custom-call | tf_op jit(solution)/shard_map/first_layer/pallas_call | solution.py:321
  72.9 0.0 copy-done
  72.9 0.0 copy-done.1
  72.9 0.0 copy-done.4
  73.0 0.0 copy-start.5
  73.0 0.0 copy-start.6
  73.0 0.0 copy-start.7
  73.0 6.0 %product_second.1 = (bf16[16,128,128]{2,1,0:T(8,128)(2,1)S(1)}, bf16[64,128,256]{2,1,0:T(8,128)(2,1)S(1)}) custom-call(s32[1,1,192]{2,1,0:T(1,128)S(1)} %copy-done.2, s32[1,1,192]{2,1,0:T(1,128)S(1)} %copy-done.3, s32[1,1]{1,0:T(1,128)S(6)} %copy.17.live, bf16[192,128,128]{2,1,0:T(8,128)(2,1)S(1)} %get-tuple-element.19.blocks, f32[64,128,128]{2,1,0:T(8,128)S(1)} %bitcast.13, ...), custom_call_target="tpu_custom_call" | custom-call | tf_op jit(solution)/shard_map/product_second/pallas_call | solution.py:255
  79.0 0.0 copy-done.5
  79.0 0.0 copy-done.6
  79.0 0.0 copy-done.7
  79.1 18.7 %second_layer.1 = (bf16[256,128]{1,0:T(8,128)(2,1)S(1)}, f32[8,128]{1,0:T(8,128)S(1)}, bf16[8,2,128,128]{3,2,1,0:T(8,128)(2,1)S(1)}) custom-call(bf16[8,256,128]{2,1,0:T(8,128)(2,1)S(1)} %bitcast.18, s32[1,256]{1,0:T(1,128)S(1)} %bitcast.20, s32[1,256]{1,0:T(1,128)S(1)} %bitcast.21, f32[1,128]{1,0:T(1,128)S(1)} %bitcast.22), custom_call_target="tpu_custom_call" | custom-call | tf_op jit(solution)/shard_map/second_layer/pallas_call | solution.py:380
  97.8 6.5 %product_back.1.pay = f32[32,17,128]{2,1,0:T(8,128)S(1)} custom-call(s32[1,1,192]{2,1,0:T(1,128)S(1)} %copy-done.2, s32[1,1,192]{2,1,0:T(1,128)S(1)} %copy-done.3, s32[1,1]{1,0:T(1,128)S(6)} %copy.17.live, bf16[192,128,128]{2,1,0:T(8,128)(2,1)S(1)} %get-tuple-element.19.blocks, bf16[16,128,128]{2,1,0:T(8,128)(2,1)S(1)} %bitcast.17, ...), custom_call_target="tpu_custom_call" | custom-call | tf_op jit(solution)/shard_map/product_back/pallas_call | solution.py:255
  104.4 23.3 %weight_gradients.1.sums = f32[32,17,128]{2,1,0:T(8,128)S(1)} custom-call(f32[32,17,128]{2,1,0:T(8,128)S(1)} %product_back.1.pay), custom_call_target="tpu_custom_call" | custom-call | tf_op jit(solution)/shard_map/weight_gradients/pallas_call | solution.py:474
  127.6 0.7 outputs.1
Async XLA Ops:
  0.6 26.7 %copy-start.3 = (s32[1,1,192]{2,1,0:T(1,128)S(1)}, s32[1,1,192]{2,1,0:T(1,128)}, u32[]{:S(2)}) copy-start(s32[1,1,192]{2,1,0:T(1,128)} %cols.5) | copy-start | bytes 2308
  0.6 26.7 %copy-start.2 = (s32[1,1,192]{2,1,0:T(1,128)S(1)}, s32[1,1,192]{2,1,0:T(1,128)}, u32[]{:S(2)}) copy-start(s32[1,1,192]{2,1,0:T(1,128)} %rows.5) | copy-start | bytes 2308
  29.1 43.8 %copy-start = (bf16[256,128]{1,0:T(8,128)(2,1)S(1)}, bf16[256,128]{1,0:T(8,128)(2,1)}, u32[]{:S(2)}) copy-start(bf16[256,128]{1,0:T(8,128)(2,1)} %w_second.3) | copy-start | bytes 196612
  29.1 43.8 %copy-start.1 = (bf16[128,256]{1,0:T(8,128)(2,1)S(1)}, bf16[128,256]{1,0:T(8,128)(2,1)}, u32[]{:S(2)}) copy-start(bf16[128,256]{1,0:T(8,128)(2,1)} %w_first.1) | copy-start | bytes 196612
  29.2 43.8 %copy-start.4 = (f32[256]{0:T(256)S(1)}, f32[256]{0:T(256)}, u32[]{:S(2)}) copy-start(f32[256]{0:T(256)} %param.19) | copy-start | bytes 3076
  73.0 6.1 %copy-start.5 = (s32[256]{0:T(256)S(1)}, s32[256]{0:T(256)}, u32[]{:S(2)}) copy-start(s32[256]{0:T(256)} %param.12) | copy-start | bytes 3076
  73.0 6.1 %copy-start.6 = (s32[256]{0:T(256)S(1)}, s32[256]{0:T(256)}, u32[]{:S(2)}) copy-start(s32[256]{0:T(256)} %param.13) | copy-start | bytes 3076
  73.0 6.1 %copy-start.7 = (f32[128]{0:T(128)S(1)}, f32[128]{0:T(128)}, u32[]{:S(2)}) copy-start(f32[128]{0:T(128)} %param.21) | copy-start | bytes 1540

commit v4 on v3

--- a/solution.py
+++ b/solution.py
@@ -17,7 +17,6 @@
 UNROLL = 32
 STEP = 2048
 PIECES, STAGGER = 2, False
-ORDER = tuple((n, s) for n in range(6) for s in range(2))
 LOADS = 4
 
 
@@ -199,18 +198,7 @@
         out[i] = total[i]
 
 
-def product_second_kernel(rows, cols, live, blocks, agg, w_first, b_first, w_second, out, hidden, source, total):
-    nodes = STEP // 128
-
-    @pl.loop(0, source.shape[0] // nodes)
-    def _(i):
-        part = pl.ds(i * nodes, nodes)
-        high, low = halves(agg[part].reshape(STEP, 128))
-        pre = dot(high, w_first[...]) + dot(low, w_first[...]) + b_first[...]
-        kept = jnp.maximum(pre, 0.0).astype(BF16)
-        hidden[part] = kept.reshape(nodes, 128, 256)
-        source[part] = dot(kept, w_second[...]).astype(BF16).reshape(nodes, 128, 128)
-
+def product_second_kernel(rows, cols, live, blocks, source, out, total):
     sparse_product(False, rows, cols, live, blocks, source, total)
 
     @pl.loop(0, out.shape[0], unroll=2)
@@ -218,47 +206,17 @@
         out[i] = total[i].astype(BF16)
 
 
-def product_back_kernel(rows, cols, live, blocks, source, agg, hidden, w_second, stats, pay,
-                        total, g_first, g_second, g_bias):
+def product_back_kernel(rows, cols, live, blocks, source, total):
     sparse_product(True, rows, cols, live, blocks, source, total)
-    nodes = STEP // 128
-    w_second_t = w_second[...].astype(F32).T.astype(BF16)
-    g_first[...] = jnp.zeros(g_first.shape, F32)
-    g_second[...] = jnp.zeros(g_second.shape, F32)
-    g_bias[...] = jnp.zeros(g_bias.shape, F32)
-
-    @pl.loop(0, hidden.shape[0] // nodes)
-    def _(i):
-        part = pl.ds(i * nodes, nodes)
-        grad = total[part].reshape(STEP, 128).astype(BF16)
-        kept = hidden[part].reshape(STEP, 256)
-        d_pre = jnp.where(kept > 0, dot(grad, w_second_t), 0.0)
-        g_second[...] += dot_tn(kept, grad)
-        g_first[...] += dot_tn(agg[part].reshape(STEP, 128).astype(BF16), d_pre.astype(BF16))
-        g_bias[...] += jnp.sum(d_pre.reshape(STEP // 8, 8, 256), axis=0)
-
-    for p in range(8):
-        pay[p, 0:16] = g_first[16 * p:16 * p + 16, 0:128]
-        pay[p + 8, 0:16] = g_first[16 * p:16 * p + 16, 128:256]
-    for p in range(16):
-        pay[p + 16, 0:16] = g_second[16 * p:16 * p + 16]
-    for p in range(4, 32):
-        pay[p, 16:17] = jnp.zeros((1, 128), F32)
-    bias = jnp.sum(g_bias[...], axis=0, keepdims=True)
-    pay[0, 16:17] = stats[0:1]
-    pay[1, 16:17] = stats[1:2]
-    pay[2, 16:17] = bias[:, 0:128]
-    pay[3, 16:17] = bias[:, 128:256]
-
-
-def product_call(kernel, index, dense, out_shape, outs, scratch, name):
+
+
+def product_call(kernel, index, dense, out_shape, scratch, name):
     return pl.pallas_call(
         kernel,
         out_shape=out_shape,
         in_specs=[SM, SM] + [VM] * (2 + len(dense)),
         out_specs=jax.tree.map(lambda _: VM, out_shape),
-        scratch_shapes=scratch + [pltpu.VMEM((outs + 1, 128, 128), F32)] if name != "product_back"
-        else [pltpu.VMEM((outs + 1, 128, 128), F32)] + scratch,
+        scratch_shapes=scratch,
         compiler_params=pltpu.CompilerParams(vmem_limit_bytes=PRODUCT_LIMIT),
         name=name,
     )(*index, *dense)
@@ -301,28 +259,63 @@
             copy.wait_send()
 
 
-def first_kernel(parts, strip, inbox, outgoing, send, recv, local, gsend, grecv, glocal):
+def first_kernel(parts, w_first, b_first, w_second, strip, hidden, scaled,
+                 inbox, outgoing, send, recv, local, gsend, grecv, glocal):
     r, c, z, yl, k = place()
     to, _ = row_peers(r)
     greet([(p, c) for p in to] + [(r, n) for n in col_neighbours(z, yl, k)])
     row_sum = RowSum(parts, inbox, PIECES, send, recv, local)
     gather = Gather(outgoing, strip, PIECES, gsend, grecv, glocal)
-    for n, s in ORDER:
-        if n == 0:
-            outgoing[gather.rows * s:gather.rows * (s + 1)] = row_sum.piece(s)
-            gather.begin(s)
-        else:
+
+    def dense(slots):
+        kept = []
+        for slot in slots:
+            high, low = halves(strip[slot])
+            pre = dot(high, w_first[...]) + dot(low, w_first[...]) + b_first[...]
+            kept.append(jnp.maximum(pre, 0.0).astype(BF16))
+        products = [dot(one, w_second[...]).astype(BF16) for one in kept]
+        for slot, one, product in zip(slots, kept, products):
+            hidden[slot] = one
+            scaled[slot] = product
+
+    def of_stage(n):
+        return [gather.slot(dz, other) for dz, other, _ in (gather.STAGES[n - 1] if n else ((0, False, ""),))]
+
+    def of_twin(n):
+        slots = [slot + 1 - 2 * k for slot in of_stage(n)]
+        for slot in slots:
+            for s in range(PIECES):
+                gather.arrived(slot, s)
+        return slots
+
+    for s in range(PIECES):
+        outgoing[gather.rows * s:gather.rows * (s + 1)] = row_sum.piece(s)
+        gather.begin(s)
+    for copy in gather.kept:
+        copy.wait()
+    dense(of_stage(0))
+    for n in range(1, 6):
+        for s in range(PIECES):
             gather.stage(n, s)
-    gather.end()
+        dense(of_stage(n) + (of_twin(n - 1) if n < 5 else []))
+        if n == 4:
+            dense(of_twin(4))
+    dense(of_twin(5))
+    for copy in gather.started:
+        copy.wait_send()
     row_sum.end()
 
 
-def first_call(parts):
+def first_call(parts, w_first, b_first, w_second):
     return pl.pallas_call(
         first_kernel,
-        out_shape=jax.ShapeDtypeStruct((32, 256, 128), F32),
-        in_specs=[ANY],
-        out_specs=VM,
+        out_shape=(
+            jax.ShapeDtypeStruct((32, 256, 128), F32),
+            jax.ShapeDtypeStruct((32, 256, 256), BF16),
+            jax.ShapeDtypeStruct((32, 256, 128), BF16),
+        ),
+        in_specs=[ANY, VM, VM, VM],
+        out_specs=(VM, VM, VM),
         scratch_shapes=[
             pltpu.VMEM((8, 256, 128), F32),
             pltpu.VMEM((256, 128), F32),
@@ -332,7 +325,7 @@
         ] + gather_scratch(PIECES),
         compiler_params=pltpu.CompilerParams(collective_id=1, has_side_effects=True, vmem_limit_bytes=LIMIT),
         name="first_layer",
-    )(parts)
+    )(parts, w_first, b_first, w_second)
 
 
 def second_kernel(parts, labels, train, b_second, logits, stats, grads,
@@ -402,7 +395,38 @@
 PIECE = 17
 
 
-def last_kernel(pay, sums, box_t, half, box_p, box_z, t_send, t_recv, p_send, p_recv, z_send, z_recv):
+def weight_gradients(total, agg, hidden, w_second, stats, pay, g_first, g_second, g_bias):
+    nodes = STEP // 128
+    w_second_t = w_second[...].astype(F32).T.astype(BF16)
+    g_first[...] = jnp.zeros(g_first.shape, F32)
+    g_second[...] = jnp.zeros(g_second.shape, F32)
+    g_bias[...] = jnp.zeros(g_bias.shape, F32)
+
+    @pl.loop(0, hidden.shape[0] // nodes)
+    def _(i):
+        part = pl.ds(i * nodes, nodes)
+        grad = total[part].reshape(STEP, 128).astype(BF16)
+        kept = hidden[part].reshape(STEP, 256)
+        d_pre = jnp.where(kept > 0, dot(grad, w_second_t), 0.0)
+        g_second[...] += dot_tn(kept, grad)
+        g_first[...] += dot_tn(agg[part].reshape(STEP, 128).astype(BF16), d_pre.astype(BF16))
+        g_bias[...] += jnp.sum(d_pre.reshape(STEP // 8, 8, 256), axis=0)
+
+    for p in range(8):
+        pay[p, 0:16] = g_first[16 * p:16 * p + 16, 0:128]
+        pay[p + 8, 0:16] = g_first[16 * p:16 * p + 16, 128:256]
+    for p in range(16):
+        pay[p + 16, 0:16] = g_second[16 * p:16 * p + 16]
+    for p in range(4, 32):
+        pay[p, 16:17] = jnp.zeros((1, 128), F32)
+    bias = jnp.sum(g_bias[...], axis=0, keepdims=True)
+    pay[0, 16:17] = stats[0:1]
+    pay[1, 16:17] = stats[1:2]
+    pay[2, 16:17] = bias[:, 0:128]
+    pay[3, 16:17] = bias[:, 128:256]
+
+
+def last_kernel(total_back, agg, hidden, w_second, stats, sums, pay, g_first, g_second, g_bias, box_t, half, box_p, box_z, t_send, t_recv, p_send, p_recv, z_send, z_recv):
     r, c, z, yl, k = place()
     me, mine16 = 4 * (r % 4) + 2 * (r // 4) + yl, 16 * k
 
@@ -426,6 +450,7 @@
     others(16, me, lambda j: signal(on_plane(j)))
     twin = (r, 4 * z + 2 * yl + 1 - k)
     signal(twin)
+    weight_gradients(total_back, agg, hidden, w_second, stats, pay, g_first, g_second, g_bias)
     pl.semaphore_wait(barrier, 23)
 
     half_copy = remote(pay.at[pl.ds(16 - mine16, 16)], box_t, t_send.at[0], t_recv.at[0], *twin)
@@ -470,13 +495,17 @@
     others(16, me, lambda j: plane_back(j, me).wait_send())
 
 
-def last_call(pay):
+def last_call(*dense):
     return pl.pallas_call(
         last_kernel,
         out_shape=jax.ShapeDtypeStruct((32, PIECE, 128), F32),
-        in_specs=[VM],
+        in_specs=[VM] * 5,
         out_specs=VM,
         scratch_shapes=[
+            pltpu.VMEM((32, PIECE, 128), F32),
+            pltpu.VMEM((128, 256), F32),
+            pltpu.VMEM((256, 128), F32),
+            pltpu.VMEM((8, 256), F32),
             pltpu.VMEM((16, PIECE, 128), F32),
             pltpu.VMEM((16, PIECE, 128), F32),
             pltpu.VMEM((16, PIECE, 128), F32),
@@ -490,7 +519,7 @@
         ],
         compiler_params=pltpu.CompilerParams(collective_id=3, has_side_effects=True, vmem_limit_bytes=LIMIT),
         name="weight_gradients",
-    )(pay)
+    )(*dense)
 
 
 def finish_kernel(sums, scores, logits, loss, g_first, b_first, g_second, b_second):
@@ -529,22 +558,21 @@
     index = (adj_rows, adj_cols, adj_live, blocks)
     shape = jax.ShapeDtypeStruct
     part = product_call(
-        product_first_kernel, index, (strip.reshape(64, 128, 128),), shape((16, 128, 128), F32), 16, [], "product_first"
-    )
-    agg = first_call(part.reshape(8, 256, 128)).reshape(64, 128, 128)
-    part, hidden = product_call(
-        product_second_kernel, index, (agg, w_first, b_first.reshape(1, 256), w_second),
-        (shape((16, 128, 128), BF16), shape((64, 128, 256), BF16)), 16, [pltpu.VMEM((64, 128, 128), BF16)], "product_second",
+        product_first_kernel, index, (strip.reshape(64, 128, 128),), shape((16, 128, 128), F32), [pltpu.VMEM((17, 128, 128), F32)],
+        "product_first",
+    )
+    agg, hidden, scaled = first_call(part.reshape(8, 256, 128), w_first, b_first.reshape(1, 256), w_second)
+    part = product_call(
+        product_second_kernel, index, (scaled.reshape(64, 128, 128),), shape((16, 128, 128), BF16),
+        [pltpu.VMEM((17, 128, 128), F32)], "product_second",
     )
     scores, stats, grads = second_call(
         part.reshape(8, 256, 128), labels.reshape(1, 256), train_mask.reshape(1, 256), b_second.reshape(1, 128)
     )
-    pay = product_call(
-        product_back_kernel, index, (grads.reshape(16, 128, 128), agg, hidden, w_second, stats),
-        shape((32, PIECE, 128), F32), 64,
-        [pltpu.VMEM((128, 256), F32), pltpu.VMEM((256, 128), F32), pltpu.VMEM((8, 256), F32)], "product_back",
-    )
-    sums = last_call(pay)
+    total = product_call(
+        product_back_kernel, index, (grads.reshape(16, 128, 128),), shape((65, 128, 128), F32), [], "product_back"
+    )
+    sums = last_call(total, agg.reshape(64, 128, 128), hidden.reshape(64, 128, 256), w_second, stats)
     logits, loss, g_first, gb_first, g_second, gb_second = finish_call(sums, scores)
     return logits, loss.reshape(()), g_first, gb_first.reshape(256), g_second, gb_second.reshape(128)
 

time: 128 us -> 122 us (0.953)
  Pallas kernels: 127 us -> 121 us
    pallas_call x3, Pallas kernels: 14.3 us -> 5.42 us  [product_call(): pl.pallas_call(kernel, out_shape=out_shape, in_specs=[SM, SM] + [VM] * (2...]
    pallas_call x1, Pallas kernels: 23.3 us -> 25.7 us  [last_call(): pl.pallas_call(last_kernel, out_shape=jax.ShapeDtypeStruct((32, PIECE, 12...]
where the time goes in v4:
time: 122 us
  Pallas kernels  121 us (99%)
  between operations  1.48 us (1%)
    pallas_call x1, Pallas kernels, first_call(): pl.pallas_call(first_kernel, out_shape=(jax.ShapeDtypeStruct((32, 256, 12...  42.8 us
    pallas_call x1, Pallas kernels, gather_call(): pl.pallas_call(gather_kernel, out_shape=(jax.ShapeDtypeStruct((32,) + fea...  26 us
    pallas_call x1, Pallas kernels, last_call(): pl.pallas_call(last_kernel, out_shape=jax.ShapeDtypeStruct((32, PIECE, 12...  25.7 us
    pallas_call x1, Pallas kernels, second_call(): pl.pallas_call(second_kernel, out_shape=(jax.ShapeDtypeStruct((256, 128),...  19.8 us
    pallas_call x3, Pallas kernels, product_call(): pl.pallas_call(kernel, out_shape=out_shape, in_specs=[SM, SM] + [VM] * (2...  5.42 us

profile of v4, /device:TPU:1, one launch (start us, length us, event | category | flops | bytes accessed | tf_op | source)
XLA Modules:
  0.0 122.1 jit_solution(4153738542775098902)
XLA Ops:
  0.6 0.0 copy-start.3
  0.6 0.0 copy-start.2
  1.3 26.0 %gather_features.1 = (bf16[32,256,128]{2,1,0:T(8,128)(2,1)S(1)}, bf16[192,128,128]{2,1,0:T(8,128)(2,1)S(1)}) custom-call(bf16[256,128]{1,0:T(8,128)(2,1)} %src.1, bf16[192,128,128]{2,1,0:T(8,128)(2,1)} %bitcast.26), custom_call_target="tpu_custom_call" | custom-call | tf_op jit(solution)/shard_map/gather_features/pallas_call | solution.py:155
  27.4 0.0 copy-done.3
  27.4 0.0 copy-done.2
  27.4 0.0 copy-start
  27.4 0.0 copy-start.1
  27.4 0.0 copy-start.6
  27.4 1.7 %product_first.1 = f32[16,128,128]{2,1,0:T(8,128)S(1)} custom-call(s32[1,1,192]{2,1,0:T(1,128)S(1)} %copy-done.2, s32[1,1,192]{2,1,0:T(1,128)S(1)} %copy-done.3, s32[1,1]{1,0:T(1,128)S(6)} %copy.17.live, bf16[192,128,128]{2,1,0:T(8,128)(2,1)S(1)} %get-tuple-element.20.blocks, bf16[64,128,128]{2,1,0:T(8,128)(2,1)S(1)} %bitcast.20), custom_call_target="tpu_custom_call" | custom-call | tf_op jit(solution)/shard_map/product_first/pallas_call | solution.py:214
  29.2 0.0 copy-done
  29.2 0.0 copy-done.1
  29.2 0.0 copy-done.6
  29.2 42.8 %first_layer.1 = (f32[32,256,128]{2,1,0:T(8,128)S(1)}, bf16[32,256,256]{2,1,0:T(8,128)(2,1)S(1)}, bf16[32,256,128]{2,1,0:T(8,128)(2,1)S(1)}) custom-call(f32[8,256,128]{2,1,0:T(8,128)S(1)} %bitcast.17, bf16[128,256]{1,0:T(8,128)(2,1)S(1)} %copy-done.1, f32[1,256]{1,0:T(1,128)S(1)} %bitcast.24, bf16[256,128]{1,0:T(8,128)(2,1)S(1)} %copy-done), custom_call_target="tpu_custom_call" | custom-call | tf_op jit(solution)/shard_map/first_layer/pallas_call | solution.py:310
  72.0 0.0 copy-start.4
  72.0 0.0 copy-start.5
  72.0 0.0 copy-start.7
  72.1 1.7 %product_second.1 = bf16[16,128,128]{2,1,0:T(8,128)(2,1)S(1)} custom-call(s32[1,1,192]{2,1,0:T(1,128)S(1)} %copy-done.2, s32[1,1,192]{2,1,0:T(1,128)S(1)} %copy-done.3, s32[1,1]{1,0:T(1,128)S(6)} %copy.17.live, bf16[192,128,128]{2,1,0:T(8,128)(2,1)S(1)} %get-tuple-element.20.blocks, bf16[64,128,128]{2,1,0:T(8,128)(2,1)S(1)} %bitcast.18), custom_call_target="tpu_custom_call" | custom-call | tf_op jit(solution)/shard_map/product_second/pallas_call | solution.py:214
  73.8 0.0 copy-done.4
  73.8 0.0 copy-done.5
  73.8 0.0 copy-done.7
  73.8 19.8 %second_layer.1 = (bf16[256,128]{1,0:T(8,128)(2,1)S(1)}, f32[8,128]{1,0:T(8,128)S(1)}, bf16[8,2,128,128]{3,2,1,0:T(8,128)(2,1)S(1)}) custom-call(bf16[8,256,128]{2,1,0:T(8,128)(2,1)S(1)} %bitcast.19, s32[1,256]{1,0:T(1,128)S(1)} %bitcast.22, s32[1,256]{1,0:T(1,128)S(1)} %bitcast.23, f32[1,128]{1,0:T(1,128)S(1)} %bitcast.25), custom_call_target="tpu_custom_call" | custom-call | tf_op jit(solution)/shard_map/second_layer/pallas_call | solution.py:373
  93.7 2.0 %product_back.1.total_back = f32[65,128,128]{2,1,0:T(8,128)S(1)} custom-call(s32[1,1,192]{2,1,0:T(1,128)S(1)} %copy-done.2, s32[1,1,192]{2,1,0:T(1,128)S(1)} %copy-done.3, s32[1,1]{1,0:T(1,128)S(6)} %copy.17.live, bf16[192,128,128]{2,1,0:T(8,128)(2,1)S(1)} %get-tuple-element.20.blocks, bf16[16,128,128]{2,1,0:T(8,128)(2,1)S(1)} %bitcast.21), custom_call_target="tpu_custom_call" | custom-call | tf_op jit(solution)/shard_map/product_back/pallas_call | solution.py:214
  95.6 25.7 %weight_gradients.1.sums = f32[32,17,128]{2,1,0:T(8,128)S(1)} custom-call(f32[65,128,128]{2,1,0:T(8,128)S(1)} %product_back.1.total_back, f32[64,128,128]{2,1,0:T(8,128)S(1)} %bitcast.15, bf16[64,128,256]{2,1,0:T(8,128)(2,1)S(1)} %bitcast.16, bf16[256,128]{1,0:T(8,128)(2,1)S(1)} %copy-done, f32[8,128]{1,0:T(8,128)S(1)} %get-tuple-element.26.stats), custom_call_target="tpu_custom_call" | custom-call | tf_op jit(solution)/shard_map/weight_gradients/pallas_call | solution.py:499
  121.3 0.7 outputs.1
Async XLA Ops:
  0.6 26.7 %copy-start.3 = (s32[1,1,192]{2,1,0:T(1,128)S(1)}, s32[1,1,192]{2,1,0:T(1,128)}, u32[]{:S(2)}) copy-start(s32[1,1,192]{2,1,0:T(1,128)} %cols.5) | copy-start | bytes 2308
  0.6 26.7 %copy-start.2 = (s32[1,1,192]{2,1,0:T(1,128)S(1)}, s32[1,1,192]{2,1,0:T(1,128)}, u32[]{:S(2)}) copy-start(s32[1,1,192]{2,1,0:T(1,128)} %rows.5) | copy-start | bytes 2308
  27.4 1.8 %copy-start = (bf16[256,128]{1,0:T(8,128)(2,1)S(1)}, bf16[256,128]{1,0:T(8,128)(2,1)}, u32[]{:S(2)}) copy-start(bf16[256,128]{1,0:T(8,128)(2,1)} %w_second.3) | copy-start | bytes 196612
  27.4 1.8 %copy-start.1 = (bf16[128,256]{1,0:T(8,128)(2,1)S(1)}, bf16[128,256]{1,0:T(8,128)(2,1)}, u32[]{:S(2)}) copy-start(bf16[128,256]{1,0:T(8,128)(2,1)} %w_first.1) | copy-start | bytes 196612
  27.4 1.8 %copy-start.6 = (f32[256]{0:T(256)S(1)}, f32[256]{0:T(256)}, u32[]{:S(2)}) copy-start(f32[256]{0:T(256)} %param.19) | copy-start | bytes 3076
  72.0 1.8 %copy-start.4 = (s32[256]{0:T(256)S(1)}, s32[256]{0:T(256)}, u32[]{:S(2)}) copy-start(s32[256]{0:T(256)} %param.12) | copy-start | bytes 3076
  72.0 1.8 %copy-start.5 = (s32[256]{0:T(256)S(1)}, s32[256]{0:T(256)}, u32[]{:S(2)}) copy-start(s32[256]{0:T(256)} %param.13) | copy-start | bytes 3076
  72.0 1.8 %copy-start.7 = (f32[128]{0:T(128)S(1)}, f32[128]{0:T(128)}, u32[]{:S(2)}) copy-start(f32[128]{0:T(128)} %param.21) | copy-start | bytes 1540

commit v5 on v4

--- a/solution.py
+++ b/solution.py
@@ -15,7 +15,7 @@
 LIMIT = 32 * 1024 * 1024
 PRODUCT_LIMIT = 24 * 1024 * 1024
 UNROLL = 32
-STEP = 2048
+STEP = 4096
 PIECES, STAGGER = 2, False
 LOADS = 4
 
@@ -48,6 +48,10 @@
 def col_neighbours(z, yl, k):
     up, down = (z + 1) % 8, (z + 7) % 8
     return (4 * up + 2 * yl + k, 4 * down + 2 * yl + k, 4 * z + 2 * (1 - yl) + k, 4 * z + 2 * yl + 1 - k)
+
+
+def second_neighbours(z, yl, k):
+    return 4 * ((z + 2) % 8) + 2 * yl + k, 4 * ((z + 6) % 8) + 2 * yl + k
 
 
 def row_peers(r):
@@ -84,12 +88,22 @@
         ((-4, True, "t"),),
     )
 
+    DIRECT = (
+        ((-1, False, "at"), (1, False, "at"), (0, True, "t")),
+        ((-2, False, "uUat"), (2, False, "dat")),
+        ((-1, True, "t"), (1, True, "t"), (-2, True, "t"), (2, True, "t")),
+        ((-3, False, "at"), (3, False, "at")),
+        ((-4, False, "at"),),
+        ((-3, True, "t"), (3, True, "t"), (-4, True, "t")),
+    )
+
     def __init__(self, src, out, pieces, send, recv, local):
         self.src, self.out, self.pieces, self.send, self.recv, self.local = src, out, pieces, send, recv, local
         self.rows = src.shape[0] // pieces
         self.r, self.c, self.z, self.yl, self.k = place()
         up, down, across, twin = col_neighbours(self.z, self.yl, self.k)
-        self.to = {"u": up, "d": down, "a": across, "t": twin}
+        up2, down2 = second_neighbours(self.z, self.yl, self.k)
+        self.to = {"u": up, "d": down, "a": across, "t": twin, "U": up2, "D": down2}
         self.started, self.kept = [], []
 
     def slot(self, dz, other):
@@ -108,15 +122,15 @@
         block = self.part(slot, s)
         remote(block, block, self.send.at[0], self.recv.at[slot, s], self.r, self.to["t"]).wait_recv()
 
-    def begin(self, s):
+    def begin(self, s, targets="udat"):
         block = self.src.at[pl.ds(s * self.rows, self.rows)]
-        self.push(block, self.c, s, "udat")
+        self.push(block, self.c, s, targets)
         mine = pltpu.make_async_copy(block, self.part(self.c, s), self.local.at[s])
         mine.start()
         self.kept.append(mine)
 
-    def stage(self, n, s):
-        for dz, other, targets in self.STAGES[n - 1]:
+    def stage(self, n, s, stages=STAGES):
+        for dz, other, targets in stages[n - 1]:
             slot = self.slot(dz, other)
             self.arrived(slot, s)
             self.push(self.part(slot, s), slot, s, targets)
@@ -134,9 +148,9 @@
 
 def gather_kernel(src, blocks, out, held, load_sem, *sems):
     r, c, z, yl, k = place()
-    greet([(r, n) for n in col_neighbours(z, yl, k)])
+    greet([(r, n) for n in col_neighbours(z, yl, k) + second_neighbours(z, yl, k)])
     gather = Gather(src, out, 1, *sems)
-    gather.begin(0)
+    gather.begin(0, "audUDt")
     share = blocks.shape[0] // LOADS
     loads = [
         pltpu.make_async_copy(blocks.at[pl.ds(i * share, share)], held.at[pl.ds(i * share, share)], load_sem.at[i])
@@ -144,8 +158,8 @@
     ]
     for load in loads:
         load.start()
-    for n in range(1, 6):
-        gather.stage(n, 0)
+    for n in range(1, 7):
+        gather.stage(n, 0, gather.DIRECT)
     gather.end()
     for load in loads:
         load.wait()

time: 122 us -> 121 us (level)
  Pallas kernels: 121 us -> 119 us
    pallas_call x3, Pallas kernels: 5.42 us -> 9.83 us  [product_call(): pl.pallas_call(kernel, out_shape=out_shape, in_specs=[SM, SM] + [VM] * (2...]
    pallas_call x1, Pallas kernels: 19.8 us -> 16.5 us  [second_call(): pl.pallas_call(second_kernel, out_shape=(jax.ShapeDtypeStruct((256, 128),...]
    pallas_call x1, Pallas kernels: 26 us -> 24.4 us  [gather_call(): pl.pallas_call(gather_kernel, out_shape=(jax.ShapeDtypeStruct((32,) + fea...]
where the time goes in v5:
time: 121 us
  Pallas kernels  119 us (98%)
  between operations  1.48 us (1%)
    pallas_call x1, Pallas kernels, first_call(): pl.pallas_call(first_kernel, out_shape=(jax.ShapeDtypeStruct((32, 256, 12...  42.9 us
    pallas_call x1, Pallas kernels, last_call(): pl.pallas_call(last_kernel, out_shape=jax.ShapeDtypeStruct((32, PIECE, 12...  24.6 us
    pallas_call x1, Pallas kernels, gather_call(): pl.pallas_call(gather_kernel, out_shape=(jax.ShapeDtypeStruct((32,) + fea...  24.4 us
    pallas_call x1, Pallas kernels, second_call(): pl.pallas_call(second_kernel, out_shape=(jax.ShapeDtypeStruct((256, 128),...  16.5 us
    pallas_call x3, Pallas kernels, product_call(): pl.pallas_call(kernel, out_shape=out_shape, in_specs=[SM, SM] + [VM] * (2...  9.83 us

profile of v5, /device:TPU:1, one launch (start us, length us, event | category | flops | bytes accessed | tf_op | source)
XLA Modules:
  0.0 120.5 jit_solution(5591946894542402602)
XLA Ops:
  0.6 0.0 copy-start.3
  0.6 0.0 copy-start.2
  1.3 24.4 %gather_features.1 = (bf16[32,256,128]{2,1,0:T(8,128)(2,1)S(1)}, bf16[192,128,128]{2,1,0:T(8,128)(2,1)S(1)}) custom-call(bf16[256,128]{1,0:T(8,128)(2,1)} %src.1, bf16[192,128,128]{2,1,0:T(8,128)(2,1)} %bitcast.26), custom_call_target="tpu_custom_call" | custom-call | tf_op jit(solution)/shard_map/gather_features/pallas_call | solution.py:169
  25.7 0.0 copy-done.3
  25.7 0.0 copy-done.2
  25.7 0.0 copy-start
  25.8 0.0 copy-start.1
  25.8 0.0 copy-start.6
  25.8 3.2 %product_first.1 = f32[16,128,128]{2,1,0:T(8,128)S(1)} custom-call(s32[1,1,192]{2,1,0:T(1,128)S(1)} %copy-done.2, s32[1,1,192]{2,1,0:T(1,128)S(1)} %copy-done.3, s32[1,1]{1,0:T(1,128)S(6)} %copy.17.live, bf16[192,128,128]{2,1,0:T(8,128)(2,1)S(1)} %get-tuple-element.20.blocks, bf16[64,128,128]{2,1,0:T(8,128)(2,1)S(1)} %bitcast.20), custom_call_target="tpu_custom_call" | custom-call | tf_op jit(solution)/shard_map/product_first/pallas_call | solution.py:228
  29.0 0.0 copy-done
  29.0 0.0 copy-done.1
  29.0 0.0 copy-done.6
  29.0 42.9 %first_layer.1 = (f32[32,256,128]{2,1,0:T(8,128)S(1)}, bf16[32,256,256]{2,1,0:T(8,128)(2,1)S(1)}, bf16[32,256,128]{2,1,0:T(8,128)(2,1)S(1)}) custom-call(f32[8,256,128]{2,1,0:T(8,128)S(1)} %bitcast.17, bf16[128,256]{1,0:T(8,128)(2,1)S(1)} %copy-done.1, f32[1,256]{1,0:T(1,128)S(1)} %bitcast.24, bf16[256,128]{1,0:T(8,128)(2,1)S(1)} %copy-done), custom_call_target="tpu_custom_call" | custom-call | tf_op jit(solution)/shard_map/first_layer/pallas_call | solution.py:324
  71.9 0.0 copy-start.4
  71.9 0.0 copy-start.5
  71.9 0.0 copy-start.7
  71.9 3.2 %product_second.1 = bf16[16,128,128]{2,1,0:T(8,128)(2,1)S(1)} custom-call(s32[1,1,192]{2,1,0:T(1,128)S(1)} %copy-done.2, s32[1,1,192]{2,1,0:T(1,128)S(1)} %copy-done.3, s32[1,1]{1,0:T(1,128)S(6)} %copy.17.live, bf16[192,128,128]{2,1,0:T(8,128)(2,1)S(1)} %get-tuple-element.20.blocks, bf16[64,128,128]{2,1,0:T(8,128)(2,1)S(1)} %bitcast.18), custom_call_target="tpu_custom_call" | custom-call | tf_op jit(solution)/shard_map/product_second/pallas_call | solution.py:228
  75.1 0.0 copy-done.4
  75.1 0.0 copy-done.5
  75.1 0.0 copy-done.7
  75.1 16.5 %second_layer.1 = (bf16[256,128]{1,0:T(8,128)(2,1)S(1)}, f32[8,128]{1,0:T(8,128)S(1)}, bf16[8,2,128,128]{3,2,1,0:T(8,128)(2,1)S(1)}) custom-call(bf16[8,256,128]{2,1,0:T(8,128)(2,1)S(1)} %bitcast.19, s32[1,256]{1,0:T(1,128)S(1)} %bitcast.22, s32[1,256]{1,0:T(1,128)S(1)} %bitcast.23, f32[1,128]{1,0:T(1,128)S(1)} %bitcast.25), custom_call_target="tpu_custom_call" | custom-call | tf_op jit(solution)/shard_map/second_layer/pallas_call | solution.py:387
  91.6 3.5 %product_back.1.total_back = f32[65,128,128]{2,1,0:T(8,128)S(1)} custom-call(s32[1,1,192]{2,1,0:T(1,128)S(1)} %copy-done.2, s32[1,1,192]{2,1,0:T(1,128)S(1)} %copy-done.3, s32[1,1]{1,0:T(1,128)S(6)} %copy.17.live, bf16[192,128,128]{2,1,0:T(8,128)(2,1)S(1)} %get-tuple-element.20.blocks, bf16[16,128,128]{2,1,0:T(8,128)(2,1)S(1)} %bitcast.21), custom_call_target="tpu_custom_call" | custom-call | tf_op jit(solution)/shard_map/product_back/pallas_call | solution.py:228
  95.1 24.6 %weight_gradients.1.sums = f32[32,17,128]{2,1,0:T(8,128)S(1)} custom-call(f32[65,128,128]{2,1,0:T(8,128)S(1)} %product_back.1.total_back, f32[64,128,128]{2,1,0:T(8,128)S(1)} %bitcast.15, bf16[64,128,256]{2,1,0:T(8,128)(2,1)S(1)} %bitcast.16, bf16[256,128]{1,0:T(8,128)(2,1)S(1)} %copy-done, f32[8,128]{1,0:T(8,128)S(1)} %get-tuple-element.26.stats), custom_call_target="tpu_custom_call" | custom-call | tf_op jit(solution)/shard_map/weight_gradients/pallas_call | solution.py:513
  119.8 0.7 outputs.1
Async XLA Ops:
  0.6 25.1 %copy-start.3 = (s32[1,1,192]{2,1,0:T(1,128)S(1)}, s32[1,1,192]{2,1,0:T(1,128)}, u32[]{:S(2)}) copy-start(s32[1,1,192]{2,1,0:T(1,128)} %cols.5) | copy-start | bytes 2308
  0.6 25.1 %copy-start.2 = (s32[1,1,192]{2,1,0:T(1,128)S(1)}, s32[1,1,192]{2,1,0:T(1,128)}, u32[]{:S(2)}) copy-start(s32[1,1,192]{2,1,0:T(1,128)} %rows.5) | copy-start | bytes 2308
  25.7 3.2 %copy-start = (bf16[256,128]{1,0:T(8,128)(2,1)S(1)}, bf16[256,128]{1,0:T(8,128)(2,1)}, u32[]{:S(2)}) copy-start(bf16[256,128]{1,0:T(8,128)(2,1)} %w_second.3) | copy-start | bytes 196612
  25.8 3.2 %copy-start.1 = (bf16[128,256]{1,0:T(8,128)(2,1)S(1)}, bf16[128,256]{1,0:T(8,128)(2,1)}, u32[]{:S(2)}) copy-start(bf16[128,256]{1,0:T(8,128)(2,1)} %w_first.1) | copy-start | bytes 196612
  25.8 3.2 %copy-start.6 = (f32[256]{0:T(256)S(1)}, f32[256]{0:T(256)}, u32[]{:S(2)}) copy-start(f32[256]{0:T(256)} %param.19) | copy-start | bytes 3076
  71.9 3.2 %copy-start.4 = (s32[256]{0:T(256)S(1)}, s32[256]{0:T(256)}, u32[]{:S(2)}) copy-start(s32[256]{0:T(256)} %param.12) | copy-start | bytes 3076
  71.9 3.2 %copy-start.5 = (s32[256]{0:T(256)S(1)}, s32[256]{0:T(256)}, u32[]{:S(2)}) copy-start(s32[256]{0:T(256)} %param.13) | copy-start | bytes 3076
  71.9 3.2 %copy-start.7 = (f32[128]{0:T(128)S(1)}, f32[128]{0:T(128)}, u32[]{:S(2)}) copy-start(f32[128]{0:T(128)} %param.21) | copy-start | bytes 1540

commit v6 on v5

--- a/solution.py
+++ b/solution.py
@@ -273,8 +273,8 @@
             copy.wait_send()
 
 
-def first_kernel(parts, w_first, b_first, w_second, strip, hidden, scaled,
-                 inbox, outgoing, send, recv, local, gsend, grecv, glocal):
+def first_kernel(parts, w_first, b_first, w_second, rounded, hidden, scaled,
+                 strip, inbox, outgoing, send, recv, local, gsend, grecv, glocal):
     r, c, z, yl, k = place()
     to, _ = row_peers(r)
     greet([(p, c) for p in to] + [(r, n) for n in col_neighbours(z, yl, k)])
@@ -285,6 +285,7 @@
         kept = []
         for slot in slots:
             high, low = halves(strip[slot])
+            rounded[slot] = high
             pre = dot(high, w_first[...]) + dot(low, w_first[...]) + b_first[...]
             kept.append(jnp.maximum(pre, 0.0).astype(BF16))
         products = [dot(one, w_second[...]).astype(BF16) for one in kept]
@@ -324,13 +325,14 @@
     return pl.pallas_call(
         first_kernel,
         out_shape=(
-            jax.ShapeDtypeStruct((32, 256, 128), F32),
+            jax.ShapeDtypeStruct((32, 256, 128), BF16),
             jax.ShapeDtypeStruct((32, 256, 256), BF16),
             jax.ShapeDtypeStruct((32, 256, 128), BF16),
         ),
         in_specs=[ANY, VM, VM, VM],
         out_specs=(VM, VM, VM),
         scratch_shapes=[
+            pltpu.VMEM((32, 256, 128), F32),
             pltpu.VMEM((8, 256, 128), F32),
             pltpu.VMEM((256, 128), F32),
             pltpu.SemaphoreType.DMA((7, PIECES)),
@@ -423,7 +425,7 @@
         kept = hidden[part].reshape(STEP, 256)
         d_pre = jnp.where(kept > 0, dot(grad, w_second_t), 0.0)
         g_second[...] += dot_tn(kept, grad)
-        g_first[...] += dot_tn(agg[part].reshape(STEP, 128).astype(BF16), d_pre.astype(BF16))
+        g_first[...] += dot_tn(agg[part].reshape(STEP, 128), d_pre.astype(BF16))
         g_bias[...] += jnp.sum(d_pre.reshape(STEP // 8, 8, 256), axis=0)
 
     for p in range(8):

time: 121 us -> 120 us (level)
    pallas_call x1, Pallas kernels: 24.6 us -> 23.1 us  [last_call(): pl.pallas_call(last_kernel, out_shape=jax.ShapeDtypeStruct((32, PIECE, 12...]
where the time goes in v6:
time: 120 us
  Pallas kernels  118 us (98%)
  between operations  1.48 us (1%)
    pallas_call x1, Pallas kernels, first_call(): pl.pallas_call(first_kernel, out_shape=(jax.ShapeDtypeStruct((32, 256, 12...  42.6 us
    pallas_call x1, Pallas kernels, gather_call(): pl.pallas_call(gather_kernel, out_shape=(jax.ShapeDtypeStruct((32,) + fea...  24.4 us
    pallas_call x1, Pallas kernels, last_call(): pl.pallas_call(last_kernel, out_shape=jax.ShapeDtypeStruct((32, PIECE, 12...  23.1 us
    pallas_call x1, Pallas kernels, second_call(): pl.pallas_call(second_kernel, out_shape=(jax.ShapeDtypeStruct((256, 128),...  17.5 us
    pallas_call x3, Pallas kernels, product_call(): pl.pallas_call(kernel, out_shape=out_shape, in_specs=[SM, SM] + [VM] * (2...  9.93 us

profile of v6, /device:TPU:1, one launch (start us, length us, event | category | flops | bytes accessed | tf_op | source)
XLA Modules:
  0.0 119.8 jit_solution(14884146579058358919)
XLA Ops:
  0.6 0.0 copy-start.3
  0.6 0.0 copy-start.2
  1.3 24.4 %gather_features.1 = (bf16[32,256,128]{2,1,0:T(8,128)(2,1)S(1)}, bf16[192,128,128]{2,1,0:T(8,128)(2,1)S(1)}) custom-call(bf16[256,128]{1,0:T(8,128)(2,1)} %src.1, bf16[192,128,128]{2,1,0:T(8,128)(2,1)} %bitcast.26), custom_call_target="tpu_custom_call" | custom-call | tf_op jit(solution)/shard_map/gather_features/pallas_call | solution.py:169
  25.7 0.0 copy-done.3
  25.7 0.0 copy-done.2
  25.7 0.0 copy-start
  25.8 0.0 copy-start.1
  25.8 0.0 copy-start.6
  25.8 3.3 %product_first.1 = f32[16,128,128]{2,1,0:T(8,128)S(1)} custom-call(s32[1,1,192]{2,1,0:T(1,128)S(1)} %copy-done.2, s32[1,1,192]{2,1,0:T(1,128)S(1)} %copy-done.3, s32[1,1]{1,0:T(1,128)S(6)} %copy.17.live, bf16[192,128,128]{2,1,0:T(8,128)(2,1)S(1)} %get-tuple-element.20.blocks, bf16[64,128,128]{2,1,0:T(8,128)(2,1)S(1)} %bitcast.20), custom_call_target="tpu_custom_call" | custom-call | tf_op jit(solution)/shard_map/product_first/pallas_call | solution.py:228
  29.1 0.0 copy-done
  29.1 0.0 copy-done.1
  29.1 0.0 copy-done.6
  29.1 42.6 %first_layer.1 = (bf16[32,256,128]{2,1,0:T(8,128)(2,1)S(1)}, bf16[32,256,256]{2,1,0:T(8,128)(2,1)S(1)}, bf16[32,256,128]{2,1,0:T(8,128)(2,1)S(1)}) custom-call(f32[8,256,128]{2,1,0:T(8,128)S(1)} %bitcast.16, bf16[128,256]{1,0:T(8,128)(2,1)S(1)} %copy-done.1, f32[1,256]{1,0:T(1,128)S(1)} %bitcast.24, bf16[256,128]{1,0:T(8,128)(2,1)S(1)} %copy-done), custom_call_target="tpu_custom_call" | custom-call | tf_op jit(solution)/shard_map/first_layer/pallas_call | solution.py:325
  71.7 0.0 copy-start.4
  71.7 0.0 copy-start.5
  71.7 0.0 copy-start.7
  71.7 3.2 %product_second.1 = bf16[16,128,128]{2,1,0:T(8,128)(2,1)S(1)} custom-call(s32[1,1,192]{2,1,0:T(1,128)S(1)} %copy-done.2, s32[1,1,192]{2,1,0:T(1,128)S(1)} %copy-done.3, s32[1,1]{1,0:T(1,128)S(6)} %copy.17.live, bf16[192,128,128]{2,1,0:T(8,128)(2,1)S(1)} %get-tuple-element.20.blocks, bf16[64,128,128]{2,1,0:T(8,128)(2,1)S(1)} %bitcast.18), custom_call_target="tpu_custom_call" | custom-call | tf_op jit(solution)/shard_map/product_second/pallas_call | solution.py:228
  74.9 0.0 copy-done.4
  74.9 0.0 copy-done.5
  74.9 0.0 copy-done.7
  74.9 17.5 %second_layer.1 = (bf16[256,128]{1,0:T(8,128)(2,1)S(1)}, f32[8,128]{1,0:T(8,128)S(1)}, bf16[8,2,128,128]{3,2,1,0:T(8,128)(2,1)S(1)}) custom-call(bf16[8,256,128]{2,1,0:T(8,128)(2,1)S(1)} %bitcast.19, s32[1,256]{1,0:T(1,128)S(1)} %bitcast.22, s32[1,256]{1,0:T(1,128)S(1)} %bitcast.23, f32[1,128]{1,0:T(1,128)S(1)} %bitcast.25), custom_call_target="tpu_custom_call" | custom-call | tf_op jit(solution)/shard_map/second_layer/pallas_call | solution.py:389
  92.5 3.5 %product_back.1.total_back = f32[65,128,128]{2,1,0:T(8,128)S(1)} custom-call(s32[1,1,192]{2,1,0:T(1,128)S(1)} %copy-done.2, s32[1,1,192]{2,1,0:T(1,128)S(1)} %copy-done.3, s32[1,1]{1,0:T(1,128)S(6)} %copy.17.live, bf16[192,128,128]{2,1,0:T(8,128)(2,1)S(1)} %get-tuple-element.20.blocks, bf16[16,128,128]{2,1,0:T(8,128)(2,1)S(1)} %bitcast.21), custom_call_target="tpu_custom_call" | custom-call | tf_op jit(solution)/shard_map/product_back/pallas_call | solution.py:228
  96.0 23.1 %weight_gradients.1.sums = f32[32,17,128]{2,1,0:T(8,128)S(1)} custom-call(f32[65,128,128]{2,1,0:T(8,128)S(1)} %product_back.1.total_back, bf16[64,128,128]{2,1,0:T(8,128)(2,1)S(1)} %bitcast.17, bf16[64,128,256]{2,1,0:T(8,128)(2,1)S(1)} %bitcast.15, bf16[256,128]{1,0:T(8,128)(2,1)S(1)} %copy-done, f32[8,128]{1,0:T(8,128)S(1)} %get-tuple-element.26.stats), custom_call_target="tpu_custom_call" | custom-call | tf_op jit(solution)/shard_map/weight_gradients/pallas_call | solution.py:515
  119.1 0.7 outputs.1
Async XLA Ops:
  0.6 25.1 %copy-start.3 = (s32[1,1,192]{2,1,0:T(1,128)S(1)}, s32[1,1,192]{2,1,0:T(1,128)}, u32[]{:S(2)}) copy-start(s32[1,1,192]{2,1,0:T(1,128)} %cols.5) | copy-start | bytes 2308
  0.6 25.1 %copy-start.2 = (s32[1,1,192]{2,1,0:T(1,128)S(1)}, s32[1,1,192]{2,1,0:T(1,128)}, u32[]{:S(2)}) copy-start(s32[1,1,192]{2,1,0:T(1,128)} %rows.5) | copy-start | bytes 2308
  25.7 3.3 %copy-start = (bf16[256,128]{1,0:T(8,128)(2,1)S(1)}, bf16[256,128]{1,0:T(8,128)(2,1)}, u32[]{:S(2)}) copy-start(bf16[256,128]{1,0:T(8,128)(2,1)} %w_second.3) | copy-start | bytes 196612
  25.8 3.3 %copy-start.1 = (bf16[128,256]{1,0:T(8,128)(2,1)S(1)}, bf16[128,256]{1,0:T(8,128)(2,1)}, u32[]{:S(2)}) copy-start(bf16[128,256]{1,0:T(8,128)(2,1)} %w_first.1) | copy-start | bytes 196612
  25.8 3.3 %copy-start.6 = (f32[256]{0:T(256)S(1)}, f32[256]{0:T(256)}, u32[]{:S(2)}) copy-start(f32[256]{0:T(256)} %param.19) | copy-start | bytes 3076
  71.7 3.2 %copy-start.4 = (s32[256]{0:T(256)S(1)}, s32[256]{0:T(256)}, u32[]{:S(2)}) copy-start(s32[256]{0:T(256)} %param.12) | copy-start | bytes 3076
  71.7 3.2 %copy-start.5 = (s32[256]{0:T(256)S(1)}, s32[256]{0:T(256)}, u32[]{:S(2)}) copy-start(s32[256]{0:T(256)} %param.13) | copy-start | bytes 3076
  71.7 3.2 %copy-start.7 = (f32[128]{0:T(128)S(1)}, f32[128]{0:T(128)}, u32[]{:S(2)}) copy-start(f32[128]{0:T(128)} %param.21) | copy-start | bytes 1540
